TPU v7x, 32 devices: a whole 2x2x4 slice. The times are simulated.
32 devices in a mesh: groups: 2 (over x), rows: 8 (over z, y), cols: 2 (over core).
Axes of the slice: x: 2, y: 2, z: 4, core: 2. Of those that a mesh axis runs over, the one named last changes fastest.
Arguments:
- weather: bfloat16 [128, 512, 256], P(('groups', 'rows'), 'cols'), parts along dimension 0, may hold values from -6 to 6
- pre_scale: float32 [256], replicated, may hold values from 0.5 to 1.5
- pre_shift: float32 [256], replicated, may hold values from -2 to 2
- w_expand: bfloat16 [256, 1024], replicated, may hold values from -0.375 to 0.375
- ex_scale: float32 [1024], replicated, may hold values from 0.5 to 1.5
- ex_shift: float32 [1024], replicated, may hold values from -2 to 2
- dw_kernel: float32 [3, 3, 1024], replicated, may hold values from -2 to 2
- dw_scale: float32 [1024], replicated, may hold values from 0.5 to 1.5
- dw_shift: float32 [1024], replicated, may hold values from -2 to 2
- w_project: bfloat16 [1024, 256], replicated, may hold values from -0.1875 to 0.1875
- win_gain: float32 [256], replicated, may hold values from 0.5 to 1.5
- win_qkv: bfloat16 [256, 768], replicated, may hold values from -0.375 to 0.375
- win_out: bfloat16 [256, 256], replicated, may hold values from -0.375 to 0.375
- win_table: float32 [8, 225], replicated, may hold values from -2 to 320, as said below
- winff_gain: float32 [256], replicated, may hold values from 0.5 to 1.5
- winff_up: bfloat16 [256, 1024], replicated, may hold values from -0.375 to 0.375
- winff_down: bfloat16 [1024, 256], replicated, may hold values from -0.1875 to 0.1875
- grid_gain: float32 [256], replicated, may hold values from 0.5 to 1.5
- grid_qkv: bfloat16 [256, 768], replicated, may hold values from -0.375 to 0.375
- grid_out: bfloat16 [256, 256], replicated, may hold values from -0.375 to 0.375
- grid_table: float32 [8, 225], replicated, may hold values from -2 to 320, as said below
- gridff_gain: float32 [256], replicated, may hold values from 0.5 to 1.5
- gridff_up: bfloat16 [256, 1024], replicated, may hold values from -0.375 to 0.375
- gridff_down: bfloat16 [1024, 256], replicated, may hold values from -0.1875 to 0.1875
Outputs:
- block_out: bfloat16 [128, 512, 256], P(('groups', 'rows'), 'cols'), parts along dimension 0
There are 2 independent parts, one for each index of `groups`. A program takes and returns all parts, laid end to end along the dimension named above; an argument that names none is the same for every part. Nothing has to cross between parts.
Inputs may be any that keep to these rules, and one draw needn't show every extreme that they name: `win_table`: bias of window attention over relative offsets. In some draws each head's entries at the offsets (7, 7) and (7, 6), columns 224 and 223, reach up to 320 and differ by 1 to 3; all other entries lie within -2 to 2. `grid_table`: bias of grid attention over relative offsets. In some draws each head's entries at the offsets (7, 7) and (7, 6), columns 224 and 223, reach up to 320 and differ by 1 to 3; all other entries lie within -2 to 2.
All inputs are finite; a program needn't handle non-finite values.
Results may differ from a plain program's by a relative error of at most 0.014.
Values may be sent and summed in bfloat16 or wider, within the bound.
A program may use at most 64 MiB of HBM per device.

v0:
```python
import jax
import jax.numpy as jnp
from jax import lax
from jax.sharding import PartitionSpec as P

WIN = 8


def extended(cells, sides, width):
    for axis, dim in sides:
        count = lax.axis_size(axis)
        ends = count - 1
        head = lax.slice_in_dim(cells, 0, width, axis=dim)
        tail = lax.slice_in_dim(cells, cells.shape[dim] - width, cells.shape[dim], axis=dim)
        cells = jnp.concatenate(
            [
                lax.ppermute(tail, axis, [(i, (i + 1) % count) for i in range(ends)]),
                cells,
                lax.ppermute(head, axis, [((i + 1) % count, i) for i in range(ends)]),
            ],
            axis=dim,
        )
    return cells


def rel_bias(table, side):
    cells = jnp.arange(side * side)
    prow = cells // side
    pcol = cells % side
    offset = (prow[:, None] - prow[None, :] + side - 1) * (2 * side - 1) + (
        pcol[:, None] - pcol[None, :] + side - 1
    )
    onehot = (
        offset[:, :, None] == jnp.arange((2 * side - 1) * (2 * side - 1))[None, None, :]
    ).astype(jnp.float32)
    return jnp.einsum("qkt,ht->hqk", onehot, table, precision=lax.Precision.HIGHEST)


def layer_norm(stream, gain):
    center = stream - jnp.mean(stream, axis=-1, keepdims=True)
    spread = jnp.mean(center * center, axis=-1, keepdims=True)
    return center * lax.rsqrt(spread + 1e-05) * gain


def attend(stream, gain, w_qkv, w_out, bias):
    groups, length, width = stream.shape
    heads = bias.shape[0]
    normed = layer_norm(stream, gain).astype(jnp.bfloat16)
    qkv = jnp.einsum("gtc,cf->gtf", normed, w_qkv, preferred_element_type=jnp.float32).astype(
        jnp.bfloat16
    )
    qkv = qkv.reshape(groups, length, 3, heads, width // heads)
    scores = jnp.einsum(
        "gqhd,gkhd->ghqk", qkv[:, :, 0], qkv[:, :, 1], preferred_element_type=jnp.float32
    )
    scores = scores * (width // heads) ** (-0.5) + bias[None]
    probs = jax.nn.softmax(scores, axis=-1).astype(jnp.bfloat16)
    mixed = jnp.einsum(
        "ghqk,gkhd->gqhd", probs, qkv[:, :, 2], preferred_element_type=jnp.float32
    ).astype(jnp.bfloat16)
    mixed = mixed.reshape(groups, length, width)
    return stream + jnp.einsum("gtc,cf->gtf", mixed, w_out, preferred_element_type=jnp.float32)


def feed(stream, gain, w_up, w_down):
    normed = layer_norm(stream, gain).astype(jnp.bfloat16)
    hidden = jax.nn.gelu(
        jnp.einsum("gtc,cf->gtf", normed, w_up, preferred_element_type=jnp.float32)
    ).astype(jnp.bfloat16)
    return stream + jnp.einsum("gtf,fc->gtc", hidden, w_down, preferred_element_type=jnp.float32)


def local(
    weather,
    pre_scale,
    pre_shift,
    w_expand,
    ex_scale,
    ex_shift,
    dw_kernel,
    dw_scale,
    dw_shift,
    w_project,
    win_gain,
    win_qkv,
    win_out,
    win_table,
    winff_gain,
    winff_up,
    winff_down,
    grid_gain,
    grid_qkv,
    grid_out,
    grid_table,
    gridff_gain,
    gridff_up,
    gridff_down,
):
    tile_rows, tile_cols, width = weather.shape
    spread_width = w_expand.shape[1]
    side = WIN
    rows_count = lax.axis_size("rows")
    cols_count = lax.axis_size("cols")
    height = weather.shape[0]
    breadth = weather.shape[1]
    normed_in = (weather.astype(jnp.float32) * pre_scale + pre_shift).astype(jnp.bfloat16)
    grown = jnp.dot(
        normed_in.reshape(height * breadth, width), w_expand, preferred_element_type=jnp.float32
    )
    grown = jax.nn.gelu(grown * ex_scale + ex_shift).astype(jnp.bfloat16)
    padded = extended(grown.reshape(height, breadth, spread_width), (("rows", 0), ("cols", 1)), 1)
    total = jnp.zeros((tile_rows, tile_cols, spread_width), jnp.float32)
    for arow in range(3):
        for bcol in range(3):
            total = (
                total
                + padded[arow : arow + tile_rows, bcol : bcol + tile_cols].astype(jnp.float32)
                * dw_kernel[arow, bcol]
            )
    depth = jax.nn.gelu(total * dw_scale + dw_shift).astype(jnp.bfloat16)
    projected = jnp.dot(
        depth.reshape(tile_rows * tile_cols, spread_width),
        w_project,
        preferred_element_type=jnp.float32,
    )
    section_one = (
        weather.astype(jnp.float32) + projected.reshape(tile_rows, tile_cols, width)
    ).astype(jnp.bfloat16)
    windows = section_one.reshape(
        tile_rows // side, side, tile_cols // side, side, width
    ).transpose(0, 2, 1, 3, 4)
    windows = windows.reshape(-1, side * side, width)
    stream = attend(
        windows.astype(jnp.float32), win_gain, win_qkv, win_out, rel_bias(win_table, side)
    )
    section_three = feed(stream, winff_gain, winff_up, winff_down).astype(jnp.bfloat16)
    section_three = section_three.reshape(
        tile_rows // side, tile_cols // side, side, side, width
    ).transpose(0, 2, 1, 3, 4)
    section_three = section_three.reshape(tile_rows, tile_cols, width)
    quarter = rows_count // side
    places = side // cols_count
    residues = tile_cols // rows_count
    ordered = section_three.reshape(side, places, quarter, cols_count, residues, width).transpose(
        2, 0, 3, 1, 4, 5
    )
    ordered = ordered.reshape(rows_count, cols_count, places, residues, width)
    arrived = lax.all_to_all(
        ordered.reshape(rows_count * cols_count, places, residues, width),
        ("rows", "cols"),
        split_axis=0,
        concat_axis=0,
        tiled=True,
    )
    arrived = arrived.reshape(rows_count, cols_count, places, residues, width)
    gridded = arrived.reshape(side, quarter, cols_count, places, residues, width).transpose(
        1, 4, 0, 2, 3, 5
    )
    gridded = gridded.reshape(-1, side * side, width)
    stream = attend(
        gridded.astype(jnp.float32), grid_gain, grid_qkv, grid_out, rel_bias(grid_table, side)
    )
    finished = feed(stream, gridff_gain, gridff_up, gridff_down).astype(jnp.bfloat16)
    finished = finished.reshape(quarter, residues, side, cols_count, places, width).transpose(
        2, 0, 3, 4, 1, 5
    )
    finished = finished.reshape(rows_count, cols_count, places, residues, width)
    returned = lax.all_to_all(
        finished.reshape(rows_count * cols_count, places, residues, width),
        ("rows", "cols"),
        split_axis=0,
        concat_axis=0,
        tiled=True,
    )
    returned = returned.reshape(rows_count, cols_count, places, residues, width)
    block_out = returned.reshape(quarter, side, cols_count, places, residues, width).transpose(
        1, 3, 0, 2, 4, 5
    )
    return block_out.reshape(tile_rows, tile_cols, width)


def solution(mesh):
    return jax.shard_map(
        local,
        mesh=mesh,
        in_specs=(
            P(("groups", "rows"), "cols", None),
            P(),
            P(),
            P(),
            P(),
            P(),
            P(),
            P(),
            P(),
            P(),
            P(),
            P(),
            P(),
            P(),
            P(),
            P(),
            P(),
            P(),
            P(),
            P(),
            P(),
            P(),
            P(),
            P(),
        ),
        out_specs=P(("groups", "rows"), "cols", None),
        check_vma=False,
    )
```

profile of v0, /device:TPU:0, one launch (start us, length us, event | category | flops | bytes accessed | tf_op | source)
XLA Modules:
  0.0 200.2 jit_solution(16191927910312202800)
XLA Ops:
  0.0 1.5 fusion.55
  1.6 4.2 %fusion.9 = bf16[2048,1024]{1,0:T(8,128)(2,1)S(1)} fusion(bf16[2048,256]{1,0:T(8,128)(2,1)S(1)} %bitcast.167, bf16[256,1024]{1,0:T(8,128)(2,1)S(1)} %copy-done, f32[1024]{0:T(1024)} %param.29, f32[1024]{0:T(1024)} %param.28), kind=kOutput, calls=%fused_computation.13 | convolution fusion | flops 1096810496 | bytes 5775360 | tf_op jit(solution)/shard_map/dot_general | solution.py:107
  5.9 4.9 %collective-permute-start = (bf16[1,256,1024]{2,1,0:T(8,128)(2,1)S(1)}, bf16[1,256,1024]{2,1,0:T(8,128)(2,1)S(1)}, u32[]{:S(2)}, u32[]{:S(2)}) collective-permute-start(bf16[1,256,1024]{2,1,0:T(8,128)(2,1)S(1)} %get-tuple-element.9), channel_id=1, source_target_pairs={{0,2},{2,4},{4,6},{6,8},{8,10},{10,12},{12,14},{1,3},{3,5},{5,7},{... | collective-permute-start | bytes 1572872 | tf_op jit(solution)/shard_map/ppermute | solution.py:17
  10.8 1.3 collective-permute-start.1
  12.3 3.2 %fusion.80 = f32[8,64,64]{2,0,1:T(8,128)S(1)} fusion(s32[64,64]{1,0:T(8,128)S(1)} %add_add_fusion, f32[8,225]{1,0:T(8,128)S(1)} %copy-done.22), kind=kOutput, calls=%fused_computation.102 | convolution fusion | flops 89395200 | bytes 154656 | tf_op jit(solution)/shard_map/qkt,ht->hqk/dot_general | solution.py:36
  15.5 17.7 %collective-permute-done = bf16[1,256,1024]{2,1,0:T(8,128)(2,1)S(1)} collective-permute-done((bf16[1,256,1024]{2,1,0:T(8,128)(2,1)S(1)}, bf16[1,256,1024]{2,1,0:T(8,128)(2,1)S(1)}, u32[]{:S(2)}, u32[]{:S(2)}) %collective-permute-start) | collective-permute-done | bytes 524320 | tf_op jit(solution)/shard_map/ppermute | solution.py:17
  34.6 1.5 collective-permute-start.3
  37.7 11.5 %maximum_maximum_fusion = (bf16[10,257,1024]{2,1,0:T(8,128)(2,1)}, bf16[10,257,1024]{2,1,0:T(8,128)(2,1)}) fusion(bf16[1,256,1024]{2,1,0:T(8,128)(2,1)S(1)} %collective-permute-done.1, bf16[8,256,1024]{2,1,0:T(8,128)(2,1)} %bitcast.154, bf16[1,256,1024]{2,1,0:T(8,128)(2,1)S(1)} %collective-permute-done, bf16[10,1,1024]{2,1,0:T(2,128)(2,1)S(1)} %collective-permute-done.2, ...), kind=kLoop, calls=%fused_computation.46 | loop fusion | flops 42106880 | bytes 15810560 | tf_op jit(solution)/shard_map/concatenate | solution.py:15
  49.3 18.7 %fusion.132 = (f32[32,8,8]{2,0,1:T(8,128)S(1)}, f32[1,32,8,8,256]{4,3,1,2,0:T(8,128)S(1)}) fusion(bf16[1024,256]{1,0:T(8,128)(2,1)S(1)} %copy-done.19, bf16[8,256,1024]{2,1,0:T(8,128)(2,1)S(1)} %bitcast.155, bf16[10,257,1024]{2,1,0:T(8,128)(2,1)} %get-tuple-element.6, bf16[1,256,1024]{2,1,0:T(8,128)(2,1)S(1)} %collective-permute-done.1, ...), kind=kOutput, calls=%fused_computation.164 | convolution fusion | flops 1158150144 | bytes 34131968 | tf_op jit(solution)/shard_map/dot_general | solution.py:121
  69.1 3.8 %convolution_convert_fusion.1 = bf16[32,64,768]{2,1,0:T(8,128)(2,1)} fusion(f32[1,32,8,8,256]{4,3,1,2,0:T(8,128)S(1)} %get-tuple-element.23, f32[256]{0:T(256)} %param.34, f32[32,64]{1,0:T(8,128)S(1)} %copy.122, f32[32,64]{1,0:T(8,128)S(1)} %copy.119, bf16[256,768]{1,0:T(8,128)(2,1)} %param.35), kind=kOutput, calls=%fused_computation.67 | convolution fusion | flops 808976384 | bytes 5653504 | tf_op jit(solution)/shard_map/gtc,cf->gtf/dot_general | solution.py:49
  72.8 6.7 %copy.123 = bf16[32,64,768]{1,2,0:T(8,128)(2,1)} copy(bf16[32,64,768]{2,1,0:T(8,128)(2,1)} %convolution_convert_fusion.1) | data formatting | bytes 6291456 | tf_op jit(solution)/shard_map/convert_element_type | solution.py:49
  79.5 3.5 %fusion.58 = f32[32,8,64,64]{2,3,1,0:T(8,128)S(1)} fusion(bf16[32,64,3,8,32]{1,4,3,2,0:T(8,128)(2,1)} %bitcast.156), kind=kOutput, calls=%fused_computation.76 | convolution fusion | flops 67108864 | bytes 8388608 | tf_op jit(solution)/shard_map/gqhd,gkhd->ghqk/dot_general | solution.py:53
  83.0 2.7 %fusion.133 = (f32[32,8,64]{2,1,0:T(8,128)S(1)}, f32[32,8,64,64]{2,3,1,0:T(8,128)S(1)}) fusion(f32[32,8,64,64]{2,3,1,0:T(8,128)S(1)} %fusion.58, f32[8,64,64]{1,2,0:T(8,128)S(1)} %copy.127), kind=kOutput, calls=%fused_computation.165 | output fusion | flops 6291519 | bytes 8585216 | tf_op jit(solution)/shard_map/sub | solution.py:57
  85.8 2.9 %fusion.65 = bf16[32,8,32,64]{3,2,1,0:T(8,128)(2,1)S(1)} fusion(f32[32,8,64,64]{2,3,1,0:T(8,128)S(1)} %get-tuple-element.25, f32[32,8,64]{2,1,0:T(8,128)S(1)} %get-tuple-element.24, bf16[32,64,3,8,32]{1,4,3,2,0:T(8,128)(2,1)} %bitcast.157), kind=kOutput, calls=%fused_computation.98 | convolution fusion | flops 69730304 | bytes 7405568 | tf_op jit(solution)/shard_map/ghqk,gkhd->gqhd/dot_general | solution.py:58
  89.7 1.3 copy-done.4
  91.7 5.3 %fusion.72 = bf16[1,32,8,8,256]{4,3,2,1,0:T(8,128)(2,1)S(1)} fusion(f32[32,64,256]{2,1,0:T(8,128)} %copy-done.4, f32[256]{0:T(256)S(1)} %copy-done.26, f32[32,64]{1,0:T(8,128)S(1)} %add_rsqrt_fusion.2, f32[32,64]{1,0:T(8,128)S(1)} %broadcast_multiply_fusion.3, bf16[1024,256]{1,0:T(8,128)(2,1)S(1)} %copy-done.20, bf16[256,1024]{1,0:T(8,128)(2,1)} %param.39), kind=kOutput, calls=%fused_computation.100 | convolution fusion | flops 2169503744 | bytes 4211712 | tf_op jit(solution)/shard_map/gtf,fc->gtc/dot_general | solution.py:70
  98.2 7.5 %all-to-all-start = ((bf16[16,4,32,256]{3,2,1,0:T(8,128)(2,1)}), bf16[16,4,32,256]{3,2,1,0:T(8,128)(2,1)}, u32[]{:S(2)}, u32[]{:S(2)}) async-start(bf16[16,4,32,256]{3,2,1,0:T(8,128)(2,1)} %bitcast.36), calls=%async_computation | async-start | bytes 2097152 | tf_op jit(solution)/shard_map/all_to_all | solution.py:148
  105.7 3.2 %fusion.81 = f32[8,64,64]{2,0,1:T(8,128)S(1)} fusion(s32[64,64]{1,0:T(8,128)S(1)} %copy-done.11, f32[8,225]{1,0:T(8,128)S(1)} %copy-done.23), kind=kOutput, calls=%fused_computation.103 | convolution fusion | flops 89395200 | bytes 154656 | tf_op jit(solution)/shard_map/qkt,ht->hqk/dot_general | solution.py:36
  109.1 19.6 %all-to-all-done = bf16[16,4,32,256]{3,2,1,0:T(8,128)(2,1)} async-done(((bf16[16,4,32,256]{3,2,1,0:T(8,128)(2,1)}), bf16[16,4,32,256]{3,2,1,0:T(8,128)(2,1)}, u32[]{:S(2)}, u32[]{:S(2)}) %all-to-all-start) | async-done | bytes 1048608 | tf_op jit(solution)/shard_map/all_to_all | solution.py:148
  128.7 1.5 bitcast_convert_fusion
  130.2 1.6 fusion.130
  131.8 2.7 %copy.167 = f32[8,1,2,4,32,256]{5,3,2,0,4,1:T(4,128)} copy(f32[8,1,2,4,32,256]{5,4,3,2,0,1:T(8,128)S(1)} %bitcast_convert_fusion) | data formatting | bytes 4194304 | tf_op jit(solution)/shard_map/convert_element_type | solution.py:161
  135.0 2.3 %multiply_reduce_fusion.1 = f32[32,8,2,4]{3,2,1,0:T(2,128)S(1)} fusion(f32[32,8,2,4]{3,2,1,0:T(2,128)S(1)} %copy.136, f32[8,1,2,4,32,256]{5,4,3,2,0,1:T(8,128)S(1)} %bitcast_convert_fusion), kind=kLoop, calls=%fused_computation.90 | loop fusion | flops 1570816 | bytes 2113536 | tf_op jit(solution)/shard_map/reduce_sum | solution.py:41
  137.5 2.0 reshape.258
  139.6 2.7 %convolution_convert_fusion = bf16[32,64,768]{2,1,0:T(8,128)(2,1)} fusion(f32[32,64,256]{2,1,0:T(8,128)S(1)} %reshape.258, f32[256]{0:T(256)S(1)} %copy-done.18, f32[32,64]{1,0:T(8,128)S(1)} %copy.139, f32[32,64]{1,0:T(8,128)S(1)} %copy.135, bf16[256,768]{1,0:T(8,128)(2,1)S(1)} %copy-done.7), kind=kOutput, calls=%fused_computation.66 | convolution fusion | flops 808976384 | bytes 5653504 | tf_op jit(solution)/shard_map/gtc,cf->gtf/dot_general | solution.py:49
  142.3 6.7 %copy.140 = bf16[32,64,768]{1,2,0:T(8,128)(2,1)} copy(bf16[32,64,768]{2,1,0:T(8,128)(2,1)} %convolution_convert_fusion) | data formatting | bytes 6291456 | tf_op jit(solution)/shard_map/convert_element_type | solution.py:49
  149.0 3.5 %fusion.57 = f32[32,8,64,64]{2,3,1,0:T(8,128)S(1)} fusion(bf16[32,64,3,8,32]{1,4,3,2,0:T(8,128)(2,1)} %bitcast.158), kind=kOutput, calls=%fused_computation.72 | convolution fusion | flops 67108864 | bytes 8388608 | tf_op jit(solution)/shard_map/gqhd,gkhd->ghqk/dot_general | solution.py:53
  152.6 2.7 %fusion.135 = (f32[32,8,64]{2,1,0:T(8,128)S(1)}, f32[32,8,64,64]{2,3,1,0:T(8,128)S(1)}) fusion(f32[32,8,64,64]{2,3,1,0:T(8,128)S(1)} %fusion.57, f32[8,64,64]{1,2,0:T(8,128)S(1)} %copy.144), kind=kOutput, calls=%fused_computation.167 | output fusion | flops 6291519 | bytes 8585216 | tf_op jit(solution)/shard_map/sub | solution.py:57
  155.3 2.9 %fusion.64 = bf16[32,8,32,64]{3,2,1,0:T(8,128)(2,1)S(1)} fusion(f32[32,8,64,64]{2,3,1,0:T(8,128)S(1)} %get-tuple-element.29, f32[32,8,64]{2,1,0:T(8,128)S(1)} %get-tuple-element.28, bf16[32,64,3,8,32]{1,4,3,2,0:T(8,128)(2,1)} %bitcast.159), kind=kOutput, calls=%fused_computation.97 | convolution fusion | flops 69730304 | bytes 7405568 | tf_op jit(solution)/shard_map/ghqk,gkhd->gqhd/dot_general | solution.py:58
  159.2 1.3 copy-done.5
  161.2 5.5 %add_convert_fusion = bf16[32,64,256]{2,1,0:T(8,128)(2,1)S(1)} fusion(f32[32,64,256]{2,1,0:T(8,128)} %copy-done.5, f32[256]{0:T(256)S(1)} %copy-done.27, f32[32,64]{1,0:T(8,128)S(1)} %add_rsqrt_fusion.1, f32[32,64]{1,0:T(8,128)S(1)} %broadcast_multiply_fusion.2, bf16[1024,256]{1,0:T(8,128)(2,1)S(1)} %copy-done.21, bf16[256,1024]{1,0:T(8,128)(2,1)} %param.46), kind=kOutput, calls=%fused_computation.86 | convolution fusion | flops 2169503744 | bytes 4211712 | tf_op jit(solution)/shard_map/gtf,fc->gtc/dot_general | solution.py:70
  167.6 31.5 %all_to_all.10 = bf16[16,4,32,256]{3,2,1,0:T(8,128)(2,1)S(1)} all-to-all(bf16[16,4,32,256]{3,2,1,0:T(8,128)(2,1)S(1)} %bitcast.163), channel_id=1, replica_groups=mesh['groups'=2,'rows'=8,'cols'=2] {'rows','cols'}, dimensions={0} | all-to-all | bytes 2097152 | tf_op jit(solution)/shard_map/all_to_all | solution.py:168
  (95 shorter events, 11.5 us)
Async XLA Ops:
  0.0 1.6 copy-start
  1.6 10.7 %copy-start.22 = (f32[8,225]{1,0:T(8,128)S(1)}, f32[8,225]{1,0:T(8,128)}, u32[]{:S(2)}) copy-start(f32[8,225]{1,0:T(8,128)} %param.37) | copy-start | bytes 21604
  5.8 27.4 %copy-start.2 = (bf16[2048,1024]{1,0:T(8,128)(2,1)}, bf16[2048,1024]{1,0:T(8,128)(2,1)S(1)}, u32[]{:S(2)}) copy-start(bf16[2048,1024]{1,0:T(8,128)(2,1)S(1)} %fusion.9) | copy-start | bytes 12582916
  5.8 30.2 %copy-start.12 = (f32[3,3,1024]{2,1,0:T(4,128)S(1)}, f32[3,3,1024]{2,1,0:T(4,128)}, u32[]{:S(2)}) copy-start(f32[3,3,1024]{2,1,0:T(4,128)} %param.30) | copy-start | bytes 110596
  5.9 27.3 %collective-permute-start = (bf16[1,256,1024]{2,1,0:T(8,128)(2,1)S(1)}, bf16[1,256,1024]{2,1,0:T(8,128)(2,1)S(1)}, u32[]{:S(2)}, u32[]{:S(2)}) collective-permute-start(bf16[1,256,1024]{2,1,0:T(8,128)(2,1)S(1)} %get-tuple-element.9), channel_id=1, source_target_pairs={{0,2},{2,4},{4,6},{6,8},{8,10},{10,12},{12,14},{1,3},{3,5},{5,7},{... | collective-permute-start | bytes 1572872 | tf_op jit(solution)/shard_map/ppermute | solution.py:17
  10.8 22.4 %collective-permute-start.1 = (bf16[1,256,1024]{2,1,0:T(8,128)(2,1)S(1)}, bf16[1,256,1024]{2,1,0:T(8,128)(2,1)S(1)}, u32[]{:S(2)}, u32[]{:S(2)}) collective-permute-start(bf16[1,256,1024]{2,1,0:T(8,128)(2,1)S(1)} %get-tuple-element.10), channel_id=1, source_target_pairs={{2,0},{4,2},{6,4},{8,6},{10,8},{12,10},{14,12},{3,1},{5,3},{7,5},{... | collective-permute-start | bytes 1572872 | tf_op jit(solution)/shard_map/ppermute | solution.py:19
  12.2 23.8 %copy-start.10 = (s32[64,64]{1,0:T(8,128)}, s32[64,64]{1,0:T(8,128)S(1)}, u32[]{:S(2)}) copy-start(s32[64,64]{1,0:T(8,128)S(1)} %add_add_fusion) | copy-start | bytes 49156
  33.3 3.7 %collective-permute-start.2 = (bf16[10,1,1024]{2,1,0:T(2,128)(2,1)S(1)}, bf16[10,1,1024]{2,1,0:T(2,128)(2,1)S(1)}, u32[]{:S(2)}, u32[]{:S(2)}) collective-permute-start(bf16[10,1,1024]{2,1,0:T(2,128)(2,1)S(1)} %get-tuple-element.7), channel_id=1, source_target_pairs={{0,1},{2,3},{4,5},{6,7},{8,9},{10,11},{12,13},{14,15},{16,17},{18,... | collective-permute-start | bytes 61448 | tf_op jit(solution)/shard_map/ppermute | solution.py:17
  34.6 3.1 %collective-permute-start.3 = (bf16[10,1,1024]{2,1,0:T(2,128)(2,1)S(1)}, bf16[10,1,1024]{2,1,0:T(2,128)(2,1)S(1)}, u32[]{:S(2)}, u32[]{:S(2)}) collective-permute-start(bf16[10,1,1024]{2,1,0:T(2,128)(2,1)S(1)} %get-tuple-element.8), channel_id=1, source_target_pairs={{1,0},{3,2},{5,4},{7,6},{9,8},{11,10},{13,12},{15,14},{17,16},{19,... | collective-permute-start | bytes 61448 | tf_op jit(solution)/shard_map/ppermute | solution.py:19
  36.9 12.3 %copy-start.3 = (bf16[2048,1024]{1,0:T(8,128)(2,1)S(1)}, bf16[2048,1024]{1,0:T(8,128)(2,1)}, u32[]{:S(2)}) copy-start(bf16[2048,1024]{1,0:T(8,128)(2,1)} %copy-done.2) | copy-start | bytes 12582916
  36.9 12.3 %copy-start.6 = (bf16[8,256,256]{2,1,0:T(8,128)(2,1)S(1)}, bf16[8,256,256]{2,1,0:T(8,128)(2,1)}, u32[]{:S(2)}) copy-start(bf16[8,256,256]{2,1,0:T(8,128)(2,1)} %param.24) | copy-start | bytes 3145732
  36.9 12.3 %copy-start.13 = (f32[1,1,1024]{2,1,0:T(1,128)S(1)}, f32[1,1,1024]{2,1,0:T(1,128)}, u32[]{:S(2)}) copy-start(f32[1,1,1024]{2,1,0:T(1,128)} %get-tuple-element.15) | copy-start | bytes 12292
  36.9 12.3 %copy-start.14 = (f32[1,1,1024]{2,1,0:T(1,128)S(1)}, f32[1,1,1024]{2,1,0:T(1,128)}, u32[]{:S(2)}) copy-start(f32[1,1,1024]{2,1,0:T(1,128)} %get-tuple-element.16) | copy-start | bytes 12292
  36.9 12.3 %copy-start.15 = (f32[1,1,1024]{2,1,0:T(1,128)S(1)}, f32[1,1,1024]{2,1,0:T(1,128)}, u32[]{:S(2)}) copy-start(f32[1,1,1024]{2,1,0:T(1,128)} %get-tuple-element.17) | copy-start | bytes 12292
  36.9 12.3 %copy-start.16 = (f32[1,1,1024]{2,1,0:T(1,128)S(1)}, f32[1,1,1024]{2,1,0:T(1,128)}, u32[]{:S(2)}) copy-start(f32[1,1,1024]{2,1,0:T(1,128)} %get-tuple-element.18) | copy-start | bytes 12292
  36.9 12.3 %copy-start.17 = (f32[1,1,1024]{2,1,0:T(1,128)S(1)}, f32[1,1,1024]{2,1,0:T(1,128)}, u32[]{:S(2)}) copy-start(f32[1,1,1024]{2,1,0:T(1,128)} %get-tuple-element.19) | copy-start | bytes 12292
  36.9 12.3 %copy-start.19 = (bf16[1024,256]{1,0:T(8,128)(2,1)S(1)}, bf16[1024,256]{1,0:T(8,128)(2,1)}, u32[]{:S(2)}) copy-start(bf16[1024,256]{1,0:T(8,128)(2,1)} %param.33) | copy-start | bytes 1572868
  36.9 12.3 %copy-start.24 = (f32[1024]{0:T(1024)S(1)}, f32[1024]{0:T(1024)}, u32[]{:S(2)}) copy-start(f32[1024]{0:T(1024)} %param.32) | copy-start | bytes 12292
  37.0 12.3 %copy-start.25 = (f32[1024]{0:T(1024)S(1)}, f32[1024]{0:T(1024)}, u32[]{:S(2)}) copy-start(f32[1024]{0:T(1024)} %param.31) | copy-start | bytes 12292
  85.8 2.9 %copy-start.8 = (bf16[256,256]{1,0:T(8,128)(2,1)S(1)}, bf16[256,256]{1,0:T(8,128)(2,1)}, u32[]{:S(2)}) copy-start(bf16[256,256]{1,0:T(8,128)(2,1)} %param.36) | copy-start | bytes 393220
  88.7 3.0 %copy-start.20 = (bf16[1024,256]{1,0:T(8,128)(2,1)S(1)}, bf16[1024,256]{1,0:T(8,128)(2,1)}, u32[]{:S(2)}) copy-start(bf16[1024,256]{1,0:T(8,128)(2,1)} %param.40) | copy-start | bytes 1572868
  88.7 3.0 %copy-start.26 = (f32[256]{0:T(256)S(1)}, f32[256]{0:T(256)}, u32[]{:S(2)}) copy-start(f32[256]{0:T(256)} %param.38) | copy-start | bytes 3076
  89.7 1.3 copy-start.4
  97.0 8.7 %copy-start.11 = (s32[64,64]{1,0:T(8,128)S(1)}, s32[64,64]{1,0:T(8,128)}, u32[]{:S(2)}) copy-start(s32[64,64]{1,0:T(8,128)} %copy-done.10) | copy-start | bytes 49156
  97.0 8.7 %copy-start.23 = (f32[8,225]{1,0:T(8,128)S(1)}, f32[8,225]{1,0:T(8,128)}, u32[]{:S(2)}) copy-start(f32[8,225]{1,0:T(8,128)} %param.44) | copy-start | bytes 21604
  98.2 30.5 %all-to-all-start = ((bf16[16,4,32,256]{3,2,1,0:T(8,128)(2,1)}), bf16[16,4,32,256]{3,2,1,0:T(8,128)(2,1)}, u32[]{:S(2)}, u32[]{:S(2)}) async-start(bf16[16,4,32,256]{3,2,1,0:T(8,128)(2,1)} %bitcast.36), calls=%async_computation | async-start | bytes 2097152 | tf_op jit(solution)/shard_map/all_to_all | solution.py:148
  131.7 7.9 %copy-start.7 = (bf16[256,768]{1,0:T(8,128)(2,1)S(1)}, bf16[256,768]{1,0:T(8,128)(2,1)}, u32[]{:S(2)}) copy-start(bf16[256,768]{1,0:T(8,128)(2,1)} %param.42) | copy-start | bytes 1179652
  131.8 7.8 %copy-start.18 = (f32[256]{0:T(256)S(1)}, f32[256]{0:T(256)}, u32[]{:S(2)}) copy-start(f32[256]{0:T(256)} %param.41) | copy-start | bytes 3076
  155.3 2.9 %copy-start.9 = (bf16[256,256]{1,0:T(8,128)(2,1)S(1)}, bf16[256,256]{1,0:T(8,128)(2,1)}, u32[]{:S(2)}) copy-start(bf16[256,256]{1,0:T(8,128)(2,1)} %param.43) | copy-start | bytes 393220
  158.2 3.0 %copy-start.21 = (bf16[1024,256]{1,0:T(8,128)(2,1)S(1)}, bf16[1024,256]{1,0:T(8,128)(2,1)}, u32[]{:S(2)}) copy-start(bf16[1024,256]{1,0:T(8,128)(2,1)} %param.47) | copy-start | bytes 1572868
  158.2 3.0 %copy-start.27 = (f32[256]{0:T(256)S(1)}, f32[256]{0:T(256)}, u32[]{:S(2)}) copy-start(f32[256]{0:T(256)} %param.45) | copy-start | bytes 3076
  161.2 39.0 %copy-start.1 = (bf16[256,1024]{1,0:T(8,128)(2,1)S(1)}, bf16[256,1024]{1,0:T(8,128)(2,1)}, u32[]{:S(2)}) copy-start(bf16[256,1024]{1,0:T(8,128)(2,1)} %param.27) | copy-start | bytes 1572868
  (1 other events, 1.3 us)
where the time goes:
time: 201 us; the launch traced here: 200 us
  matrix products  61.4 us (31%)
  waiting for transfers between devices  38.1 us (19%)
  blocking collectives  31.5 us (16%)
  local copies, waits for them, and re-layouts  26 us (13%)
  other arithmetic  26 us (13%)
  starting transfers between devices  16.5 us (8%)
    all_to_all x1, blocking collectives, local(): lax.all_to_all(finished.reshape(rows_count * cols_count, places, residues...  31.5 us
    all_to_all x1, waiting for transfers between devices, local(): lax.all_to_all(ordered.reshape(rows_count * cols_count, places, residues,...  19.6 us
    dot_general x1, matrix products, local(): jnp.dot(depth.reshape(tile_rows * tile_cols, spread_width), w_project, pr...  18.7 us
    ppermute x2, waiting for transfers between devices, extended(): lax.ppermute(tail, axis, [(i, (i + 1) % count) for i in range(ends)])  17.7 us
    convert_element_type x2, local copies, waits for them, and re-layouts, attend(): jnp.einsum('gtc,cf->gtf', normed, w_qkv, preferred_element_type=jnp.float32)  13.3 us
    concatenate x1, other arithmetic, extended(): jnp.concatenate([lax.ppermute(tail, axis, [(i, (i + 1) % count) for i in...  11.5 us
    dot_general x2, matrix products, feed(): jnp.einsum('gtf,fc->gtc', hidden, w_down, preferred_element_type=jnp.floa...  10.8 us
    all_to_all x1, starting transfers between devices, local(): lax.all_to_all(ordered.reshape(rows_count * cols_count, places, residues,...  7.52 us
  transfers between devices with their start and end apart: 5, of which 3 were waited for; matrix products, arithmetic and copies ran while one was open for 4% of the time, Pallas kernels for 0%

commit v1 on v0

v1 whole, which is shorter than its diff:
```python
import functools
import math

import jax
import jax.numpy as jnp
from jax import lax
from jax.experimental import pallas as pl
from jax.experimental.pallas import tpu as pltpu
from jax.sharding import PartitionSpec as P

WIN = 8
BF = jnp.bfloat16
F32 = jnp.float32
LOG2E = math.log2(math.e)
NT = (((1,), (1,)), ((), ()))
TN = (((0,), (0,)), ((), ()))


def extended(cells, sides, width):
    for axis, dim in sides:
        count = lax.axis_size(axis)
        ends = count - 1
        head = lax.slice_in_dim(cells, 0, width, axis=dim)
        tail = lax.slice_in_dim(cells, cells.shape[dim] - width, cells.shape[dim], axis=dim)
        cells = jnp.concatenate(
            [
                lax.ppermute(tail, axis, [(i, (i + 1) % count) for i in range(ends)]),
                cells,
                lax.ppermute(head, axis, [((i + 1) % count, i) for i in range(ends)]),
            ],
            axis=dim,
        )
    return cells


def bias_keys_first(table):
    heads = table.shape[0]
    grid = (table * LOG2E).reshape(heads, 2 * WIN - 1, 2 * WIN - 1)
    rows = jnp.stack([grid[:, WIN - 1 - k : 2 * WIN - 1 - k, :] for k in range(WIN)])
    both = jnp.stack(
        [rows[..., WIN - 1 - k : 2 * WIN - 1 - k] for k in range(WIN)], axis=1
    )
    return both.reshape(WIN * WIN, heads * WIN * WIN)


def gelu(x):
    c0 = math.sqrt(2.0 / math.pi)
    inner = x * (c0 + (c0 * 0.044715) * (x * x))
    half = 0.5 * x
    return half + half * jnp.tanh(inner)


def norm(x, gain):
    center = x - jnp.mean(x, axis=-1, keepdims=True)
    spread = jnp.mean(center * center, axis=-1, keepdims=True)
    return (center * lax.rsqrt(spread + 1e-05) * gain).astype(BF)


def dot(a, b):
    return jnp.dot(a, b, preferred_element_type=F32)


def attend(x, gain, w_qk, w_vt, w_out, bias):
    width = x.shape[1]
    cells = WIN * WIN
    groups = x.shape[0] // cells
    heads = bias.shape[1] // cells
    dim = width // heads
    scale = dim ** (-0.5) * LOG2E
    n = norm(x, gain)
    qk = dot(n, w_qk).astype(BF)
    vt = lax.dot_general(w_vt, n, NT, preferred_element_type=F32).astype(BF)
    lane_head = lax.broadcasted_iota(jnp.int32, (cells, width), 1) // dim
    probs = []
    for g in range(groups):
        q = qk[g * cells : (g + 1) * cells, :width]
        k = qk[g * cells : (g + 1) * cells, width:]
        spread = jnp.concatenate(
            [jnp.where(lane_head == h, q, jnp.zeros_like(q)) for h in range(heads)], axis=0
        )
        s = lax.dot_general(k, spread, NT, preferred_element_type=F32) * scale + bias
        e = jnp.exp2(s - jnp.max(s, axis=0, keepdims=True))
        e = e * (1.0 / jnp.sum(e, axis=0, keepdims=True))
        probs.append(e.astype(BF))
    low = lax.broadcasted_iota(jnp.int32, (dim, 2 * cells), 1) < cells
    zeros = jnp.zeros((cells, 2 * cells), BF)
    mixed = []
    for g in range(0, groups, 2):
        parts = []
        for t in range(heads // 2):
            at = slice(2 * cells * t, 2 * cells * (t + 1))
            pair = jnp.concatenate(
                [
                    jnp.concatenate([probs[g][:, at], zeros], axis=1),
                    jnp.concatenate([zeros, probs[g + 1][:, at]], axis=1),
                ],
                axis=0,
            )
            v = vt[2 * dim * t : 2 * dim * (t + 1), g * cells : (g + 2) * cells]
            o = dot(v, pair)
            a, b = o[:, : 2 * cells], o[:, 2 * cells :]
            parts.append(jnp.where(low, a[:dim], pltpu.roll(b[:dim], cells, 1)))
            parts.append(jnp.where(low, pltpu.roll(a[dim:], cells, 1), b[dim:]))
        mixed.append(jnp.concatenate(parts, axis=0).astype(BF))
    mixed = jnp.concatenate(mixed, axis=1)
    return x + lax.dot_general(mixed, w_out, TN, preferred_element_type=F32)


def feed(x, gain, up_ref, down_ref, step=256):
    n = norm(x, gain)
    total = x
    for at in range(0, up_ref.shape[1], step):
        hidden = gelu(dot(n, up_ref[:, at : at + step])).astype(BF)
        total = total + dot(hidden, down_ref[at : at + step, :])
    return total


PAD = 8


def first_kernel(
    valid, ext, pre_scale, pre_shift, w_expand, ex_scale, ex_shift, taps, dw_scale, dw_shift,
    w_project, gain, w_qk, w_vt, w_out, bias, ffgain, up, down, out, grown, depth, one,
):
    rows, cols, width = out.shape
    wide = w_expand.shape[1]
    span = ext.shape[1]
    column = lax.broadcasted_iota(jnp.int32, (span, 1), 0)
    edge = jnp.where(column == PAD - 1, valid[2], jnp.where(column == PAD + cols, valid[3], 1.0))

    def expand(r, carry):
        keep = jnp.where(r == 0, valid[0], jnp.where(r == rows + 1, valid[1], 1.0))
        x = (ext[r].astype(F32) * pre_scale[...] + pre_shift[...]).astype(BF)
        for at in range(0, wide, 256):
            s = slice(at, at + 256)
            y = gelu(dot(x, w_expand[:, s]) * ex_scale[:, s] + ex_shift[:, s])
            grown[r, :, s] = (y * (edge * keep)).astype(BF)
        return carry

    lax.fori_loop(0, rows + 2, expand, 0)

    def row(r, carry):
        for lane in range(0, wide, 128):
            ls = slice(lane, lane + 128)
            for c in range(0, cols, 64):
                sums = [None] * 3
                for a in range(3):
                    e = grown[r + a, c : c + 64 + 2 * PAD, ls].astype(F32)
                    for b in range(3):
                        term = e * taps[3 * a + b : 3 * a + b + 1, ls]
                        sums[b] = term if a == 0 else sums[b] + term
                total = (
                    sums[0][PAD - 1 : PAD + 63]
                    + sums[1][PAD : PAD + 64]
                    + sums[2][PAD + 1 : PAD + 65]
                )
                depth[c : c + 64, ls] = gelu(
                    total * dw_scale[:, ls] + dw_shift[:, ls]
                ).astype(BF)
        y = ext[r + 1, PAD : PAD + cols, :].astype(F32) + dot(depth[...], w_project[...])
        one[r] = y.astype(BF).astype(F32)
        return carry

    lax.fori_loop(0, rows, row, 0)

    def window(m, carry):
        pieces = []
        for g in range(4):
            at = pl.multiple_of(m * 32 + g * 8, 8)
            pieces.append(one[:, pl.ds(at, 8), :].reshape(WIN * WIN, width))
        x = jnp.concatenate(pieces, axis=0)
        x = attend(x, gain[...], w_qk[...], w_vt[...], w_out[...], bias[...])
        x = feed(x, ffgain[...], up, down)
        x = x.reshape(4, WIN, WIN, width)
        y = jnp.concatenate([x[g] for g in range(4)], axis=1)
        out[:, pl.ds(pl.multiple_of(m * 32, 32), 32), :] = y.astype(BF)
        return carry

    lax.fori_loop(0, cols // 32, window, 0)


def second_kernel(x_ref, gain, w_qk, w_vt, w_out, bias, ffgain, up, down, out):
    def group(m, carry):
        at = pl.ds(pl.multiple_of(m * 256, 256), 256)
        x = x_ref[at, :].astype(F32)
        x = attend(x, gain[...], w_qk[...], w_vt[...], w_out[...], bias[...])
        out[at, :] = feed(x, ffgain[...], up, down).astype(BF)
        return carry

    lax.fori_loop(0, x_ref.shape[0] // 256, group, 0)


def attention_operands(gain, w_qkv, w_out, table):
    width = w_qkv.shape[0]
    return (
        gain[None],
        w_qkv[:, : 2 * width],
        w_qkv[:, 2 * width :].T,
        w_out,
        bias_keys_first(table),
    )


def local(
    weather, pre_scale, pre_shift, w_expand, ex_scale, ex_shift, dw_kernel, dw_scale, dw_shift,
    w_project, win_gain, win_qkv, win_out, win_table, winff_gain, winff_up, winff_down,
    grid_gain, grid_qkv, grid_out, grid_table, gridff_gain, gridff_up, gridff_down,
):
    tile_rows, tile_cols, width = weather.shape
    wide = w_expand.shape[1]
    side = WIN
    rows_count = lax.axis_size("rows")
    cols_count = lax.axis_size("cols")
    ext = extended(weather, (("rows", 0), ("cols", 1)), 1)
    ext = jnp.pad(ext, ((0, 0), (PAD - 1, PAD - 1), (0, 0)))
    ri, ci = lax.axis_index("rows"), lax.axis_index("cols")
    valid = jnp.stack([ri > 0, ri < rows_count - 1, ci > 0, ci < cols_count - 1]).astype(F32)
    vmem = pl.BlockSpec(memory_space=pltpu.VMEM)
    section_three = pl.pallas_call(
        first_kernel,
        out_shape=jax.ShapeDtypeStruct((tile_rows, tile_cols, width), BF),
        in_specs=[pl.BlockSpec(memory_space=pltpu.SMEM)] + [vmem] * 18,
        out_specs=vmem,
        scratch_shapes=[
            pltpu.VMEM((tile_rows + 2, tile_cols + 2 * PAD, wide), BF),
            pltpu.VMEM((tile_cols, wide), BF),
            pltpu.VMEM((tile_rows, tile_cols, width), F32),
        ],
        compiler_params=pltpu.CompilerParams(vmem_limit_bytes=50 << 20),
        name="mbconv_window",
    )(
        valid, ext, pre_scale[None], pre_shift[None], w_expand, ex_scale[None], ex_shift[None],
        dw_kernel.reshape(9, wide), dw_scale[None], dw_shift[None], w_project,
        *attention_operands(win_gain, win_qkv, win_out, win_table),
        winff_gain[None], winff_up, winff_down,
    )
    quarter = rows_count // side
    places = side // cols_count
    residues = tile_cols // rows_count
    ordered = section_three.reshape(side, places, quarter, cols_count, residues, width).transpose(
        2, 0, 3, 1, 4, 5
    )
    arrived = lax.all_to_all(
        ordered.reshape(rows_count * cols_count, places, residues, width),
        ("rows", "cols"),
        split_axis=0,
        concat_axis=0,
        tiled=True,
    )
    gridded = arrived.reshape(side, quarter, cols_count, places, residues, width).transpose(
        1, 4, 0, 2, 3, 5
    )
    finished = pl.pallas_call(
        second_kernel,
        out_shape=jax.ShapeDtypeStruct((tile_rows * tile_cols, width), BF),
        in_specs=[vmem] * 9,
        out_specs=vmem,
        compiler_params=pltpu.CompilerParams(vmem_limit_bytes=50 << 20),
        name="grid",
    )(
        gridded.reshape(-1, width),
        *attention_operands(grid_gain, grid_qkv, grid_out, grid_table),
        gridff_gain[None], gridff_up, gridff_down,
    )
    finished = finished.reshape(quarter, residues, side, cols_count, places, width).transpose(
        2, 0, 3, 4, 1, 5
    )
    returned = lax.all_to_all(
        finished.reshape(rows_count * cols_count, places, residues, width),
        ("rows", "cols"),
        split_axis=0,
        concat_axis=0,
        tiled=True,
    )
    block_out = returned.reshape(quarter, side, cols_count, places, residues, width).transpose(
        1, 3, 0, 2, 4, 5
    )
    return block_out.reshape(tile_rows, tile_cols, width)


def solution(mesh):
    spread = P(("groups", "rows"), "cols", None)
    return jax.shard_map(
        local,
        mesh=mesh,
        in_specs=(spread,) + (P(),) * 23,
        out_specs=spread,
        check_vma=False,
    )
```

time: 201 us -> 152 us (0.76)
  matrix products: 61.4 us -> 0 us
  Pallas kernels: 0 us -> 53.7 us
  other arithmetic: 26 us -> 4.19 us
  waiting for transfers between devices: 38.1 us -> 19.7 us
    dot_general x14 -> x0, matrix products: 61.4 us -> none  [the longest x1 18.7 us: local(): jnp.dot(depth.reshape(tile_rows * tile_cols, spread_width), w_project, pr...]
    pallas_call x0 -> x2, Pallas kernels: none -> 53.7 us  [the longest x1 38.1 us: local(): pl.pallas_call(first_kernel, out_shape=jax.ShapeDtypeStruct((tile_rows, t...]
    convert_element_type x4 -> x0, local copies, waits for them, and re-layouts: 18 us -> none  [the longest x2 13.3 us: attend(): jnp.einsum('gtc,cf->gtf', normed, w_qkv, preferred_element_type=jnp.float32)]
    ppermute x2, waiting for transfers between devices: 17.7 us -> 0.01 us  [extended(): lax.ppermute(tail, axis, [(i, (i + 1) % count) for i in range(ends)])]
    concatenate x1, other arithmetic: 11.5 us -> 2.7 us  [extended(): jnp.concatenate([lax.ppermute(tail, axis, [(i, (i + 1) % count) for i in...]
    unnamed x56 -> x78, local copies, waits for them, and re-layouts: 2.78 us -> 11.4 us
    reshape x1 -> x8, local copies, waits for them, and re-layouts: 0.07 us -> 6.05 us  [the longest x2 2.38 us: bias_keys_first(): return both.reshape(WIN * WIN, heads * WIN * WIN)]
    reduce_sum x5 -> x0, other arithmetic: 5.82 us -> none  [the longest x4 4.23 us: layer_norm(): spread = jnp.mean(center * center, axis=-1, keepdims=True)]
  transfers between devices with their start and end apart: 5 -> 5, of which waited for: 3 -> 1; matrix products, arithmetic and copies ran while one was open for 4% -> 11% of each run, Pallas kernels for 0% -> 0%
where the time goes in v1:
time: 152 us; the launch traced here: 151 us
  Pallas kernels  53.7 us (35%)
  blocking collectives  31.5 us (21%)
  local copies, waits for them, and re-layouts  24.6 us (16%)
  waiting for transfers between devices  19.7 us (13%)
  starting transfers between devices  16.6 us (11%)
  other arithmetic  4.19 us (3%)
    pallas_call x1, Pallas kernels, local(): pl.pallas_call(first_kernel, out_shape=jax.ShapeDtypeStruct((tile_rows, t...  38.1 us
    all_to_all x1, blocking collectives, local(): lax.all_to_all(finished.reshape(rows_count * cols_count, places, residues...  31.5 us
    all_to_all x1, waiting for transfers between devices, local(): lax.all_to_all(ordered.reshape(rows_count * cols_count, places, residues,...  19.7 us
    pallas_call x1, Pallas kernels, local(): pl.pallas_call(second_kernel, out_shape=jax.ShapeDtypeStruct((tile_rows *...  15.6 us
    unnamed x78, local copies, waits for them, and re-layouts  11.4 us
    all_to_all x1, starting transfers between devices, local(): lax.all_to_all(ordered.reshape(rows_count * cols_count, places, residues,...  7.68 us
    ppermute x2, starting transfers between devices, extended(): lax.ppermute(tail, axis, [(i, (i + 1) % count) for i in range(ends)])  6.34 us
  transfers between devices with their start and end apart: 5, of which 1 were waited for; matrix products, arithmetic and copies ran while one was open for 11% of the time, Pallas kernels for 0%

profile of v1, /device:TPU:0, one launch (start us, length us, event | category | flops | bytes accessed | tf_op | source)
XLA Modules:
  0.0 151.0 jit_solution(7991550850619911347)
XLA Ops:
  0.0 1.0 fusion.23
  1.0 4.9 %collective-permute-start = (bf16[1,256,256]{2,1,0:T(8,128)(2,1)S(1)}, bf16[1,256,256]{2,1,0:T(8,128)(2,1)S(1)}, u32[]{:S(2)}, u32[]{:S(2)}) collective-permute-start(bf16[1,256,256]{2,1,0:T(8,128)(2,1)S(1)} %get-tuple-element.8), channel_id=1, source_target_pairs={{0,2},{2,4},{4,6},{6,8},{8,10},{10,12},{12,14},{1,3},{3,5},{5,7},{... | collective-permute-start | bytes 393224 | tf_op jit(solution)/shard_map/ppermute | solution.py:27
  5.9 1.3 collective-permute-start.1
  7.2 0.7 broadcast_multiply_fusion
  8.1 0.7 broadcast_multiply_fusion.1
  9.0 0.8 fusion.21
  9.8 0.8 fusion.20
  10.6 0.8 fusion.19
  11.5 0.8 fusion.18
  12.3 0.8 fusion.17
  13.2 0.8 fusion.16
  14.0 0.9 fusion.15
  14.8 0.7 fusion.14
  16.3 1.1 constant_dynamic-update-slice_fusion.1
  18.0 0.8 fusion.22
  18.8 1.5 collective-permute-start.2
  20.3 1.3 collective-permute-start.3
  21.7 1.7 %copy.49 = f32[8,8,8,8,8]{4,3,2,1,0:T(8,128)S(1)} copy(f32[8,8,8,8,8]{4,3,2,0,1:T(8,128)} %fusion.14) | data formatting | bytes 262144 | tf_op jit(solution)/shard_map/stack | solution.py:40
  23.5 1.2 reshape.41.bias
  25.0 2.7 %fusion.5.ext = bf16[10,272,256]{2,1,0:T(8,128)(2,1)} fusion(bf16[10,1,256]{2,1,0:T(2,128)(2,1)S(1)} %collective-permute-done.3, bf16[10,256,256]{2,1,0:T(8,128)(2,1)} %constant_dynamic-update-slice_fusion, bf16[10,1,256]{2,1,0:T(2,128)(2,1)S(1)} %collective-permute-done.2), kind=kLoop, calls=%fused_computation.7 | loop fusion | flops 8355840 | bytes 2713600 | tf_op jit(solution)/shard_map/concatenate | solution.py:25
  27.8 38.1 %mbconv_window.1 = bf16[8,256,256]{2,1,0:T(8,128)(2,1)S(1)} custom-call(f32[4]{0:T(128)S(1)} %add_convert_fusion.valid, bf16[10,272,256]{2,1,0:T(8,128)(2,1)} %fusion.5.ext, f32[1,256]{1,0:T(1,128)S(1)} %bitcast.169, f32[1,256]{1,0:T(1,128)S(1)} %bitcast.170, bf16[256,1024]{1,0:T(8,128)(2,1)S(1)} %copy-done, f32[1,1024]{1,0:T(1,128)S(1)} %bitcast.165, ...), custom_call_target="tpu_custom_call" | custom-call | tf_op jit(solution)/shard_map/mbconv_window/pallas_call | solution.py:219
  65.9 1.1 copy.50
  67.0 7.7 %all-to-all-start = ((bf16[16,4,32,256]{3,2,1,0:T(8,128)(2,1)}), bf16[16,4,32,256]{3,2,1,0:T(8,128)(2,1)}, u32[]{:S(2)}, u32[]{:S(2)}) async-start(bf16[16,4,32,256]{3,2,1,0:T(8,128)(2,1)} %bitcast.31), calls=%async_computation | async-start | bytes 2097152 | tf_op jit(solution)/shard_map/all_to_all | solution.py:243
  76.0 1.2 reshape.47.bias
  77.2 0.8 copy.57
  77.9 19.7 %all-to-all-done = bf16[16,4,32,256]{3,2,1,0:T(8,128)(2,1)} async-done(((bf16[16,4,32,256]{3,2,1,0:T(8,128)(2,1)}), bf16[16,4,32,256]{3,2,1,0:T(8,128)(2,1)}, u32[]{:S(2)}, u32[]{:S(2)}) %all-to-all-start) | async-done | bytes 1048608 | tf_op jit(solution)/shard_map/all_to_all | solution.py:243
  97.7 2.1 %copy.59 = bf16[8,1,2,4,32,256]{5,3,2,0,4,1:T(4,128)(2,1)S(1)} copy(bf16[8,1,2,4,32,256]{5,4,3,2,0,1:T(8,128)(2,1)} %bitcast.32) | data formatting | bytes 2097152 | tf_op jit(solution)/shard_map/reshape | solution.py:250
  100.1 0.9 copy-done.6
  101.0 0.9 copy-done.8
  101.9 15.6 %grid.1 = bf16[2048,256]{1,0:T(8,128)(2,1)S(1)} custom-call(bf16[2048,256]{1,0:T(8,128)(2,1)S(1)} %reshape.45.x_ref, f32[1,256]{1,0:T(1,128)S(1)} %bitcast.173, bf16[256,512]{1,0:T(8,128)(2,1)S(1)} %slice.142.w_qk, bf16[256,256]{1,0:T(8,128)(2,1)S(1)} %bitcast.164, bf16[256,256]{1,0:T(8,128)(2,1)S(1)} %copy-done.8, f32[64,512]{1,0:T(8,128)S(1)} %reshape.47.bias, ...), custom_call_target="tpu_custom_call" | custom-call | tf_op jit(solution)/shard_map/grid/pallas_call | solution.py:253
  118.5 31.5 %all_to_all.10 = bf16[16,4,32,256]{3,2,1,0:T(8,128)(2,1)S(1)} all-to-all(bf16[16,4,32,256]{3,2,1,0:T(8,128)(2,1)S(1)} %bitcast.177), channel_id=1, replica_groups=mesh['groups'=2,'rows'=8,'cols'=2] {'rows','cols'}, dimensions={0} | all-to-all | bytes 2097152 | tf_op jit(solution)/shard_map/all_to_all | solution.py:268
  150.0 1.1 copy.55
  (89 shorter events, 4.3 us)
Async XLA Ops:
  1.0 14.6 %collective-permute-start = (bf16[1,256,256]{2,1,0:T(8,128)(2,1)S(1)}, bf16[1,256,256]{2,1,0:T(8,128)(2,1)S(1)}, u32[]{:S(2)}, u32[]{:S(2)}) collective-permute-start(bf16[1,256,256]{2,1,0:T(8,128)(2,1)S(1)} %get-tuple-element.8), channel_id=1, source_target_pairs={{0,2},{2,4},{4,6},{6,8},{8,10},{10,12},{12,14},{1,3},{3,5},{5,7},{... | collective-permute-start | bytes 393224 | tf_op jit(solution)/shard_map/ppermute | solution.py:27
  5.9 11.5 %collective-permute-start.1 = (bf16[1,256,256]{2,1,0:T(8,128)(2,1)S(1)}, bf16[1,256,256]{2,1,0:T(8,128)(2,1)S(1)}, u32[]{:S(2)}, u32[]{:S(2)}) collective-permute-start(bf16[1,256,256]{2,1,0:T(8,128)(2,1)S(1)} %get-tuple-element.7), channel_id=1, source_target_pairs={{2,0},{4,2},{6,4},{8,6},{10,8},{12,10},{14,12},{3,1},{5,3},{7,5},{... | collective-permute-start | bytes 393224 | tf_op jit(solution)/shard_map/ppermute | solution.py:29
  9.8 6.5 %copy-start.19 = (bf16[8,256,256]{2,1,0:T(8,128)(2,1)S(1)}, bf16[8,256,256]{2,1,0:T(8,128)(2,1)}, u32[]{:S(2)}) copy-start(bf16[8,256,256]{2,1,0:T(8,128)(2,1)} %param.24) | copy-start | bytes 3145732
  14.0 7.7 %copy-start.21 = (bf16[256,768]{1,0:T(8,128)(2,1)S(1)}, bf16[256,768]{1,0:T(8,128)(2,1)}, u32[]{:S(2)}) copy-start(bf16[256,768]{1,0:T(8,128)(2,1)} %param.35) | copy-start | bytes 1179652
  18.8 6.1 %collective-permute-start.2 = (bf16[10,1,256]{2,1,0:T(2,128)(2,1)S(1)}, bf16[10,1,256]{2,1,0:T(2,128)(2,1)S(1)}, u32[]{:S(2)}, u32[]{:S(2)}) collective-permute-start(bf16[10,1,256]{2,1,0:T(2,128)(2,1)S(1)} %get-tuple-element.5), channel_id=1, source_target_pairs={{0,1},{2,3},{4,5},{6,7},{8,9},{10,11},{12,13},{14,15},{16,17},{18,... | collective-permute-start | bytes 15368 | tf_op jit(solution)/shard_map/ppermute | solution.py:27
  20.3 4.7 %collective-permute-start.3 = (bf16[10,1,256]{2,1,0:T(2,128)(2,1)S(1)}, bf16[10,1,256]{2,1,0:T(2,128)(2,1)S(1)}, u32[]{:S(2)}, u32[]{:S(2)}) collective-permute-start(bf16[10,1,256]{2,1,0:T(2,128)(2,1)S(1)} %get-tuple-element.6), channel_id=1, source_target_pairs={{1,0},{3,2},{5,4},{7,6},{9,8},{11,10},{13,12},{15,14},{17,16},{19,... | collective-permute-start | bytes 15368 | tf_op jit(solution)/shard_map/ppermute | solution.py:29
  23.4 1.2 slice-start.1
  23.4 1.5 copy-start.22
  24.6 3.0 %copy-start = (bf16[256,1024]{1,0:T(8,128)(2,1)S(1)}, bf16[256,1024]{1,0:T(8,128)(2,1)}, u32[]{:S(2)}) copy-start(bf16[256,1024]{1,0:T(8,128)(2,1)} %w_expand.1) | copy-start | bytes 1572868
  24.7 3.0 %copy-start.1 = (bf16[1024,256]{1,0:T(8,128)(2,1)S(1)}, bf16[1024,256]{1,0:T(8,128)(2,1)}, u32[]{:S(2)}) copy-start(bf16[1024,256]{1,0:T(8,128)(2,1)} %w_project.1) | copy-start | bytes 1572868
  24.7 3.0 %copy-start.2 = (bf16[256,1024]{1,0:T(8,128)(2,1)S(1)}, bf16[256,1024]{1,0:T(8,128)(2,1)}, u32[]{:S(2)}) copy-start(bf16[256,1024]{1,0:T(8,128)(2,1)} %up.2) | copy-start | bytes 1572868
  24.7 3.0 %copy-start.3 = (bf16[1024,256]{1,0:T(8,128)(2,1)S(1)}, bf16[1024,256]{1,0:T(8,128)(2,1)}, u32[]{:S(2)}) copy-start(bf16[1024,256]{1,0:T(8,128)(2,1)} %down.2) | copy-start | bytes 1572868
  24.7 3.0 %copy-start.7 = (bf16[256,256]{1,0:T(8,128)(2,1)S(1)}, bf16[256,256]{1,0:T(8,128)(2,1)}, u32[]{:S(2)}) copy-start(bf16[256,256]{1,0:T(8,128)(2,1)} %w_out.2) | copy-start | bytes 393220
  24.7 3.0 %copy-start.9 = (f32[1024]{0:T(1024)S(1)}, f32[1024]{0:T(1024)}, u32[]{:S(2)}) copy-start(f32[1024]{0:T(1024)} %param.28) | copy-start | bytes 12292
  24.7 3.0 %copy-start.10 = (f32[1024]{0:T(1024)S(1)}, f32[1024]{0:T(1024)}, u32[]{:S(2)}) copy-start(f32[1024]{0:T(1024)} %param.29) | copy-start | bytes 12292
  24.7 3.0 %copy-start.11 = (f32[1024]{0:T(1024)S(1)}, f32[1024]{0:T(1024)}, u32[]{:S(2)}) copy-start(f32[1024]{0:T(1024)} %param.31) | copy-start | bytes 12292
  24.7 3.0 %copy-start.12 = (f32[1024]{0:T(1024)S(1)}, f32[1024]{0:T(1024)}, u32[]{:S(2)}) copy-start(f32[1024]{0:T(1024)} %param.32) | copy-start | bytes 12292
  24.8 3.0 %copy-start.13 = (f32[256]{0:T(256)S(1)}, f32[256]{0:T(256)}, u32[]{:S(2)}) copy-start(f32[256]{0:T(256)} %param.25) | copy-start | bytes 3076
  24.8 3.0 %copy-start.14 = (f32[256]{0:T(256)S(1)}, f32[256]{0:T(256)}, u32[]{:S(2)}) copy-start(f32[256]{0:T(256)} %param.26) | copy-start | bytes 3076
  24.8 3.0 %copy-start.15 = (f32[256]{0:T(256)S(1)}, f32[256]{0:T(256)}, u32[]{:S(2)}) copy-start(f32[256]{0:T(256)} %param.34) | copy-start | bytes 3076
  24.8 3.0 %copy-start.16 = (f32[256]{0:T(256)S(1)}, f32[256]{0:T(256)}, u32[]{:S(2)}) copy-start(f32[256]{0:T(256)} %param.38) | copy-start | bytes 3076
  65.9 8.8 %copy-start.20 = (bf16[256,768]{1,0:T(8,128)(2,1)S(1)}, bf16[256,768]{1,0:T(8,128)(2,1)}, u32[]{:S(2)}) copy-start(bf16[256,768]{1,0:T(8,128)(2,1)} %param.42) | copy-start | bytes 1179652
  67.0 30.7 %all-to-all-start = ((bf16[16,4,32,256]{3,2,1,0:T(8,128)(2,1)}), bf16[16,4,32,256]{3,2,1,0:T(8,128)(2,1)}, u32[]{:S(2)}, u32[]{:S(2)}) async-start(bf16[16,4,32,256]{3,2,1,0:T(8,128)(2,1)} %bitcast.31), calls=%async_computation | async-start | bytes 2097152 | tf_op jit(solution)/shard_map/all_to_all | solution.py:243
  76.0 1.2 slice-start
  97.7 2.4 %copy-start.4 = (bf16[256,1024]{1,0:T(8,128)(2,1)S(1)}, bf16[256,1024]{1,0:T(8,128)(2,1)}, u32[]{:S(2)}) copy-start(bf16[256,1024]{1,0:T(8,128)(2,1)} %up.3) | copy-start | bytes 1572868
  97.7 2.4 %copy-start.5 = (bf16[1024,256]{1,0:T(8,128)(2,1)S(1)}, bf16[1024,256]{1,0:T(8,128)(2,1)}, u32[]{:S(2)}) copy-start(bf16[1024,256]{1,0:T(8,128)(2,1)} %down.3) | copy-start | bytes 1572868
  97.7 2.5 %copy-start.17 = (f32[256]{0:T(256)S(1)}, f32[256]{0:T(256)}, u32[]{:S(2)}) copy-start(f32[256]{0:T(256)} %param.41) | copy-start | bytes 3076
  97.7 2.5 %copy-start.18 = (f32[256]{0:T(256)S(1)}, f32[256]{0:T(256)}, u32[]{:S(2)}) copy-start(f32[256]{0:T(256)} %param.45) | copy-start | bytes 3076
  100.1 0.9 copy-start.6
  101.0 0.9 copy-start.8

commit v2 on v1

--- a/solution.py
+++ b/solution.py
@@ -33,14 +33,18 @@
     return cells
 
 
-def bias_keys_first(table):
-    heads = table.shape[0]
-    grid = (table * LOG2E).reshape(heads, 2 * WIN - 1, 2 * WIN - 1)
-    rows = jnp.stack([grid[:, WIN - 1 - k : 2 * WIN - 1 - k, :] for k in range(WIN)])
-    both = jnp.stack(
-        [rows[..., WIN - 1 - k : 2 * WIN - 1 - k] for k in range(WIN)], axis=1
+def biases_keys_first(tables):
+    count, heads, offsets = tables.shape
+    cells = WIN * WIN
+    pair = jnp.arange(cells * cells)
+    k, q = pair // cells, pair % cells
+    offset = (q // WIN - k // WIN + WIN - 1) * (2 * WIN - 1) + (q % WIN - k % WIN + WIN - 1)
+    onehot = (jnp.arange(offsets)[:, None] == offset[None, :]).astype(F32)
+    flat = jnp.dot(
+        tables.reshape(count * heads, offsets) * LOG2E, onehot, precision=lax.Precision.HIGHEST
     )
-    return both.reshape(WIN * WIN, heads * WIN * WIN)
+    flat = flat.reshape(count, heads, cells, cells).transpose(0, 2, 1, 3)
+    return flat.reshape(count, cells, heads * cells)
 
 
 def gelu(x):
@@ -118,10 +122,54 @@
 PAD = 8
 
 
-def first_kernel(
+def block_kernel(
     valid, ext, pre_scale, pre_shift, w_expand, ex_scale, ex_shift, taps, dw_scale, dw_shift,
-    w_project, gain, w_qk, w_vt, w_out, bias, ffgain, up, down, out, grown, depth, one,
+    w_project, gain, w_qk, w_vt, w_out, bias, ffgain, up, down, gain2, w_qk2, w_vt2, w_out2,
+    bias2, ffgain2, up2, down2, out, grown, depth, one, sent, arrived, returned, back, loose,
+    sent_sem, arrived_sem, returned_sem, back_sem, *, quarter,
 ):
+    row_at, col_at = lax.axis_index("rows"), lax.axis_index("cols")
+    col_count = lax.axis_size("cols")
+    peers = WIN * col_count
+    me = (row_at // quarter) * col_count + col_at
+
+    def place(peer):
+        return {
+            "rows": (peer // col_count) * quarter + lax.rem(row_at, quarter),
+            "cols": lax.rem(peer, col_count),
+        }
+
+    barrier = pltpu.get_barrier_semaphore()
+
+    def greet(k, carry):
+        pl.semaphore_signal(
+            barrier, 1, device_id=place(lax.rem(me + k, peers)),
+            device_id_type=pl.DeviceIdType.MESH,
+        )
+        return carry
+
+    lax.fori_loop(1, peers, greet, 0)
+
+    def send(m, src, dst, src_sem, dst_sem):
+        def one_peer(k, carry):
+            peer = lax.rem(me + k, peers)
+            pltpu.make_async_remote_copy(
+                src_ref=src.at[m, peer],
+                dst_ref=dst.at[m, me],
+                send_sem=src_sem.at[m],
+                recv_sem=dst_sem.at[m],
+                device_id=place(peer),
+                device_id_type=pl.DeviceIdType.MESH,
+            ).start()
+            return carry
+
+        lax.fori_loop(1, peers, one_peer, 0)
+        dst[m, me] = src[m, me]
+
+    def wait_all(m, ref, sem):
+        part = ref.at[m, pl.ds(0, peers - 1)]
+        pltpu.make_async_copy(part, part, sem.at[m]).wait()
+
     rows, cols, width = out.shape
     wide = w_expand.shape[1]
     span = ext.shape[1]
@@ -163,41 +211,96 @@
 
     lax.fori_loop(0, rows, row, 0)
 
+    pl.semaphore_wait(barrier, peers - 1)
+    first_half = lax.rem(lax.broadcasted_iota(jnp.int32, (WIN * WIN, width), 0), WIN) < WIN // 2
+    half = WIN // 2
+    chunks = cols // 32
+
+    def exchange(a, b):
+        firsts = jnp.where(first_half, a, pltpu.roll(b, half, 0))
+        seconds = jnp.where(first_half, pltpu.roll(a, WIN * WIN - half, 0), b)
+        return firsts, seconds
+
     def window(m, carry):
         pieces = []
         for g in range(4):
-            at = pl.multiple_of(m * 32 + g * 8, 8)
-            pieces.append(one[:, pl.ds(at, 8), :].reshape(WIN * WIN, width))
+            at = pl.multiple_of(g * (cols // 4) + m * WIN, WIN)
+            pieces.append(one[:, pl.ds(at, WIN), :].reshape(WIN * WIN, width))
         x = jnp.concatenate(pieces, axis=0)
         x = attend(x, gain[...], w_qk[...], w_vt[...], w_out[...], bias[...])
         x = feed(x, ffgain[...], up, down)
-        x = x.reshape(4, WIN, WIN, width)
-        y = jnp.concatenate([x[g] for g in range(4)], axis=1)
-        out[:, pl.ds(pl.multiple_of(m * 32, 32), 32), :] = y.astype(BF)
-        return carry
-
-    lax.fori_loop(0, cols // 32, window, 0)
-
-
-def second_kernel(x_ref, gain, w_qk, w_vt, w_out, bias, ffgain, up, down, out):
+        x = [x[WIN * WIN * g : WIN * WIN * (g + 1)] for g in range(4)]
+        low, high = exchange(x[0], x[1]), exchange(x[2], x[3])
+        for c in range(2):
+            y = jnp.concatenate(
+                [low[c].reshape(WIN, WIN, width), high[c].reshape(WIN, WIN, width)], axis=1
+            ).astype(BF)
+            for i in range(WIN):
+                sent[m, i * 2 + c] = y[i]
+        send(m, sent, arrived, sent_sem, arrived_sem)
+        return carry
+
+    lax.fori_loop(0, chunks, window, 0)
+
     def group(m, carry):
-        at = pl.ds(pl.multiple_of(m * 256, 256), 256)
-        x = x_ref[at, :].astype(F32)
-        x = attend(x, gain[...], w_qk[...], w_vt[...], w_out[...], bias[...])
-        out[at, :] = feed(x, ffgain[...], up, down).astype(BF)
-        return carry
-
-    lax.fori_loop(0, x_ref.shape[0] // 256, group, 0)
-
-
-def attention_operands(gain, w_qkv, w_out, table):
+        wait_all(m, arrived, arrived_sem)
+        loose_x = arrived[m].astype(F32).reshape(256, width)
+        for h in range(width // 128):
+            loose[h] = loose_x[:, 128 * h : 128 * (h + 1)]
+        x = jnp.concatenate(
+            [
+                jnp.concatenate([loose[h, pl.ds(g, 64, stride=4), :] for h in range(width // 128)], axis=1)
+                for g in range(4)
+            ],
+            axis=0,
+        )
+        x = attend(x, gain2[...], w_qk2[...], w_vt2[...], w_out2[...], bias2[...])
+        x = feed(x, ffgain2[...], up2, down2)
+        for g in range(4):
+            for h in range(width // 128):
+                loose[h, pl.ds(g, 64, stride=4), :] = x[64 * g : 64 * (g + 1), 128 * h : 128 * (h + 1)]
+        y = jnp.concatenate([loose[h] for h in range(width // 128)], axis=1)
+        returned[m] = y.reshape(peers, 16, width).astype(BF)
+        send(m, returned, back, returned_sem, back_sem)
+        return carry
+
+    lax.fori_loop(0, chunks, group, 0)
+
+    def finish(n, carry):
+        cols_of = [[], [], [], []]
+        for d in range(2):
+            m = 2 * n + d
+            wait_all(m, back, back_sem)
+            y = back[m].astype(F32).reshape(WIN, 2, 2, WIN, width)
+            for pp in range(2):
+                halves = exchange(
+                    y[:, 0, pp].reshape(WIN * WIN, width), y[:, 1, pp].reshape(WIN * WIN, width)
+                )
+                for e in range(2):
+                    cols_of[2 * pp + e].append(halves[e].reshape(WIN, WIN, width))
+        for p in range(4):
+            at = pl.multiple_of(p * (cols // 4) + n * 2 * WIN, 2 * WIN)
+            out[:, pl.ds(at, 2 * WIN), :] = jnp.concatenate(cols_of[p], axis=1).astype(BF)
+        return carry
+
+    lax.fori_loop(0, chunks // 2, finish, 0)
+
+    def drain(m, carry):
+        wait_all(m, sent, sent_sem)
+        wait_all(m, returned, returned_sem)
+        return carry
+
+    lax.fori_loop(0, chunks, drain, 0)
+
+
+def attention_operands(gain, w_qkv, w_out, bias):
     width = w_qkv.shape[0]
     return (
         gain[None],
         w_qkv[:, : 2 * width],
         w_qkv[:, 2 * width :].T,
         w_out,
-        bias_keys_first(table),
+        bias,
     )
 
 
@@ -216,66 +319,37 @@
     ri, ci = lax.axis_index("rows"), lax.axis_index("cols")
     valid = jnp.stack([ri > 0, ri < rows_count - 1, ci > 0, ci < cols_count - 1]).astype(F32)
     vmem = pl.BlockSpec(memory_space=pltpu.VMEM)
-    section_three = pl.pallas_call(
-        first_kernel,
+    biases = biases_keys_first(jnp.stack([win_table, grid_table]))
+    chunks = tile_cols // 32
+    slots = pltpu.VMEM((chunks, side * cols_count, 16, width), BF)
+    return pl.pallas_call(
+        functools.partial(block_kernel, quarter=rows_count // side),
         out_shape=jax.ShapeDtypeStruct((tile_rows, tile_cols, width), BF),
-        in_specs=[pl.BlockSpec(memory_space=pltpu.SMEM)] + [vmem] * 18,
+        in_specs=[pl.BlockSpec(memory_space=pltpu.SMEM)] + [vmem] * 26,
         out_specs=vmem,
         scratch_shapes=[
             pltpu.VMEM((tile_rows + 2, tile_cols + 2 * PAD, wide), BF),
             pltpu.VMEM((tile_cols, wide), BF),
             pltpu.VMEM((tile_rows, tile_cols, width), F32),
-        ],
-        compiler_params=pltpu.CompilerParams(vmem_limit_bytes=50 << 20),
-        name="mbconv_window",
+            slots,
+            slots,
+            slots,
+            slots,
+            pltpu.VMEM((width // 128, 256, 128), F32),
+        ]
+        + [pltpu.SemaphoreType.DMA((chunks,))] * 4,
+        compiler_params=pltpu.CompilerParams(
+            vmem_limit_bytes=50 << 20, collective_id=0, has_side_effects=True
+        ),
+        name="maxvit",
     )(
         valid, ext, pre_scale[None], pre_shift[None], w_expand, ex_scale[None], ex_shift[None],
         dw_kernel.reshape(9, wide), dw_scale[None], dw_shift[None], w_project,
-        *attention_operands(win_gain, win_qkv, win_out, win_table),
+        *attention_operands(win_gain, win_qkv, win_out, biases[0]),
         winff_gain[None], winff_up, winff_down,
-    )
-    quarter = rows_count // side
-    places = side // cols_count
-    residues = tile_cols // rows_count
-    ordered = section_three.reshape(side, places, quarter, cols_count, residues, width).transpose(
-        2, 0, 3, 1, 4, 5
-    )
-    arrived = lax.all_to_all(
-        ordered.reshape(rows_count * cols_count, places, residues, width),
-        ("rows", "cols"),
-        split_axis=0,
-        concat_axis=0,
-        tiled=True,
-    )
-    gridded = arrived.reshape(side, quarter, cols_count, places, residues, width).transpose(
-        1, 4, 0, 2, 3, 5
-    )
-    finished = pl.pallas_call(
-        second_kernel,
-        out_shape=jax.ShapeDtypeStruct((tile_rows * tile_cols, width), BF),
-        in_specs=[vmem] * 9,
-        out_specs=vmem,
-        compiler_params=pltpu.CompilerParams(vmem_limit_bytes=50 << 20),
-        name="grid",
-    )(
-        gridded.reshape(-1, width),
-        *attention_operands(grid_gain, grid_qkv, grid_out, grid_table),
+        *attention_operands(grid_gain, grid_qkv, grid_out, biases[1]),
         gridff_gain[None], gridff_up, gridff_down,
     )
-    finished = finished.reshape(quarter, residues, side, cols_count, places, width).transpose(
-        2, 0, 3, 4, 1, 5
-    )
-    returned = lax.all_to_all(
-        finished.reshape(rows_count * cols_count, places, residues, width),
-        ("rows", "cols"),
-        split_axis=0,
-        concat_axis=0,
-        tiled=True,
-    )
-    block_out = returned.reshape(quarter, side, cols_count, places, residues, width).transpose(
-        1, 3, 0, 2, 4, 5
-    )
-    return block_out.reshape(tile_rows, tile_cols, width)
 
 
 def solution(mesh):

time: 152 us -> 98.8 us (0.65)
  blocking collectives: 31.5 us -> 0 us
  Pallas kernels: 53.7 us -> 75.8 us
  local copies, waits for them, and re-layouts: 24.6 us -> 5.84 us
  waiting for transfers between devices: 19.7 us -> 1.89 us
  starting transfers between devices: 16.6 us -> 9.64 us
  matrix products: 0 us -> 3.33 us
  other arithmetic: 4.19 us -> 1.4 us
    all_to_all x1 -> x0, blocking collectives: 31.5 us -> none  [local(): lax.all_to_all(finished.reshape(rows_count * cols_count, places, residues...]
    pallas_call x2 -> x1, Pallas kernels: 53.7 us -> 75.8 us  [local(): pl.pallas_call(functools.partial(block_kernel, quarter=rows_count // side...]
    all_to_all x1 -> x0, waiting for transfers between devices: 19.7 us -> none  [local(): lax.all_to_all(ordered.reshape(rows_count * cols_count, places, residues,...]
    all_to_all x1 -> x0, starting transfers between devices: 7.68 us -> none  [local(): lax.all_to_all(ordered.reshape(rows_count * cols_count, places, residues,...]
    unnamed x78 -> x47, local copies, waits for them, and re-layouts: 11.4 us -> 3.83 us
    reshape x8 -> x0, local copies, waits for them, and re-layouts: 6.32 us -> none  [the longest x2 2.38 us: bias_keys_first(): return both.reshape(WIN * WIN, heads * WIN * WIN)]
    dot_general x0 -> x1, matrix products: none -> 3.33 us  [biases_keys_first(): jnp.dot(tables.reshape(count * heads, offsets) * LOG2E, onehot, precision...]
    another operation x6 -> x0, local copies, waits for them, and re-layouts: 2.72 us -> none  [the longest x4 2.71 us: bias_keys_first(): jnp.stack([rows[..., WIN - 1 - k:2 * WIN - 1 - k] for k in range(WIN)], a...]
  transfers between devices with their start and end apart: 5 -> 4, of which waited for: 1 -> 2; matrix products, arithmetic and copies ran while one was open for 11% -> 5% of each run, Pallas kernels for 0% -> 0%
where the time goes in v2:
time: 98.8 us; the launch traced here: 98.4 us
  Pallas kernels  75.8 us (77%)
  starting transfers between devices  9.64 us (10%)
  local copies, waits for them, and re-layouts  5.84 us (6%)
  matrix products  3.33 us (3%)
  waiting for transfers between devices  1.89 us (2%)
  other arithmetic  1.4 us (1%)
    pallas_call x1, Pallas kernels, local(): pl.pallas_call(functools.partial(block_kernel, quarter=rows_count // side...  75.8 us
    ppermute x2, starting transfers between devices, extended(): lax.ppermute(tail, axis, [(i, (i + 1) % count) for i in range(ends)])  7.07 us
    unnamed x47, local copies, waits for them, and re-layouts  3.83 us
    dot_general x1, matrix products, biases_keys_first(): jnp.dot(tables.reshape(count * heads, offsets) * LOG2E, onehot, precision...  3.33 us
    ppermute x2, starting transfers between devices, extended(): lax.ppermute(head, axis, [((i + 1) % count, i) for i in range(ends)])  2.57 us
  transfers between devices with their start and end apart: 4, of which 2 were waited for; matrix products, arithmetic and copies ran while one was open for 5% of the time, Pallas kernels for 0%

profile of v2, /device:TPU:0, one launch (start us, length us, event | category | flops | bytes accessed | tf_op | source)
XLA Modules:
  0.0 98.4 jit_solution(8611444117837372392)
XLA Ops:
  0.0 1.6 %fusion.42 = (bf16[1,256,256]{2,1,0:T(8,128)(2,1)}, bf16[1,256,256]{2,1,0:T(8,128)(2,1)S(1)}) fusion(bf16[8,256,256]{2,1,0:T(8,128)(2,1)} %param.24), kind=kLoop, calls=%fused_computation.62 | loop fusion | bytes 524288 | tf_op jit(solution)/shard_map/slice | solution.py:23
  1.6 5.7 %collective-permute-start = (bf16[1,256,256]{2,1,0:T(8,128)(2,1)S(1)}, bf16[1,256,256]{2,1,0:T(8,128)(2,1)}, u32[]{:S(2)}, u32[]{:S(2)}) collective-permute-start(bf16[1,256,256]{2,1,0:T(8,128)(2,1)S(1)} %get-tuple-element.8), channel_id=1, source_target_pairs={{0,2},{2,4},{4,6},{6,8},{8,10},{10,12},{12,14},{1,3},{3,5},{5,7},{... | collective-permute-start | bytes 393224 | tf_op jit(solution)/shard_map/ppermute | solution.py:27
  7.3 1.3 %collective-permute-start.1 = (bf16[1,256,256]{2,1,0:T(8,128)(2,1)}, bf16[1,256,256]{2,1,0:T(8,128)(2,1)S(1)}, u32[]{:S(2)}, u32[]{:S(2)}) collective-permute-start(bf16[1,256,256]{2,1,0:T(8,128)(2,1)} %get-tuple-element.7), channel_id=1, source_target_pairs={{2,0},{4,2},{6,4},{8,6},{10,8},{12,10},{14,12},{3,1},{5,3},{7,5},{... | collective-permute-start | bytes 393224 | tf_op jit(solution)/shard_map/ppermute | solution.py:29
  8.6 0.1 fusion.16
  8.7 3.3 %fusion.10 = f32[2,64,8,64]{3,2,1,0:T(8,128)S(1)} fusion(s32[64,64]{1,0:T(8,128)S(1)} %fusion.16, f32[1,8,225]{2,1,0:T(8,128)} %bitcast.46, f32[1,8,225]{2,1,0:T(8,128)} %bitcast.47), kind=kOutput, calls=%fused_computation.12 | convolution fusion | flops 177876000 | bytes 292928 | tf_op jit(solution)/shard_map/dot_general | solution.py:43
  12.1 0.9 constant_dynamic-update-slice_fusion.2
  13.0 0.0 copy-start.18
  13.0 0.0 copy-start.19
  13.0 0.1 constant_dynamic-update-slice_fusion.1
  13.1 0.0 slice-start
  13.1 1.2 %collective-permute-done.1 = bf16[1,256,256]{2,1,0:T(8,128)(2,1)S(1)} collective-permute-done((bf16[1,256,256]{2,1,0:T(8,128)(2,1)}, bf16[1,256,256]{2,1,0:T(8,128)(2,1)S(1)}, u32[]{:S(2)}, u32[]{:S(2)}) %collective-permute-start.1) | collective-permute-done | bytes 131104 | tf_op jit(solution)/shard_map/ppermute | solution.py:29
  14.4 0.0 slice-start.1
  14.4 1.4 %collective-permute-start.2 = (bf16[10,1,256]{2,1,0:T(2,128)(2,1)S(1)}, bf16[10,1,256]{2,1,0:T(2,128)(2,1)S(1)}, u32[]{:S(2)}, u32[]{:S(2)}) collective-permute-start(bf16[10,1,256]{2,1,0:T(2,128)(2,1)S(1)} %get-tuple-element.5), channel_id=1, source_target_pairs={{0,1},{2,3},{4,5},{6,7},{8,9},{10,11},{12,13},{14,15},{16,17},{18,... | collective-permute-start | bytes 15368 | tf_op jit(solution)/shard_map/ppermute | solution.py:27
  15.8 1.3 %collective-permute-start.3 = (bf16[10,1,256]{2,1,0:T(2,128)(2,1)S(1)}, bf16[10,1,256]{2,1,0:T(2,128)(2,1)S(1)}, u32[]{:S(2)}, u32[]{:S(2)}) collective-permute-start(bf16[10,1,256]{2,1,0:T(2,128)(2,1)S(1)} %get-tuple-element.6), channel_id=1, source_target_pairs={{1,0},{3,2},{5,4},{7,6},{9,8},{11,10},{13,12},{15,14},{17,16},{19,... | collective-permute-start | bytes 15368 | tf_op jit(solution)/shard_map/ppermute | solution.py:29
  17.1 0.1 add_convert_fusion.valid
  17.3 0.1 squeeze.6.bias
  17.4 0.1 squeeze.7.bias2
  17.5 0.1 copy.28
  17.7 0.1 copy.29
  17.8 0.3 copy-done.20
  18.1 0.0 copy-start.1
  18.1 0.0 copy-start.2
  18.1 0.0 copy-start.7
  18.1 0.0 copy-start.8
  18.2 0.0 copy-start.11
  18.2 0.0 copy-start.12
  18.2 0.0 copy-start.15
  18.2 0.0 copy-start.16
  18.2 0.7 collective-permute-done.3
  18.9 1.2 %fusion.9.ext = bf16[10,272,256]{2,1,0:T(8,128)(2,1)} fusion(bf16[10,1,256]{2,1,0:T(2,128)(2,1)S(1)} %collective-permute-done.3, bf16[10,256,256]{2,1,0:T(8,128)(2,1)S(1)} %constant_dynamic-update-slice_fusion, bf16[10,1,256]{2,1,0:T(2,128)(2,1)S(1)} %collective-permute-done.2), kind=kLoop, calls=%fused_computation.11 | loop fusion | flops 8355840 | bytes 2713600 | tf_op jit(solution)/shard_map/concatenate | solution.py:25
  20.3 75.8 %maxvit.1 = bf16[8,256,256]{2,1,0:T(8,128)(2,1)} custom-call(f32[4]{0:T(128)S(1)} %add_convert_fusion.valid, bf16[10,272,256]{2,1,0:T(8,128)(2,1)} %fusion.9.ext, f32[1,256]{1,0:T(1,128)S(1)} %bitcast.40, f32[1,256]{1,0:T(1,128)S(1)} %bitcast.41, bf16[256,1024]{1,0:T(8,128)(2,1)S(1)} %copy-done, f32[1,1024]{1,0:T(1,128)S(1)} %bitcast.36, ...), custom_call_target="tpu_custom_call" | custom-call | tf_op jit(solution)/shard_map/maxvit/pallas_call | solution.py:325
  96.1 2.3 %copy.33 = bf16[8,256,256]{2,1,0:T(8,128)(2,1)} copy(bf16[8,256,256]{2,1,0:T(8,128)(2,1)} %maxvit.1) | data formatting | bytes 2097152
  (41 shorter events, 0.2 us)
Async XLA Ops:
  1.6 11.4 %copy-start.17 = (bf16[8,256,256]{2,1,0:T(8,128)(2,1)S(1)}, bf16[8,256,256]{2,1,0:T(8,128)(2,1)}, u32[]{:S(2)}) copy-start(bf16[8,256,256]{2,1,0:T(8,128)(2,1)} %param.24) | copy-start | bytes 3145732
  1.6 10.4 %collective-permute-start = (bf16[1,256,256]{2,1,0:T(8,128)(2,1)S(1)}, bf16[1,256,256]{2,1,0:T(8,128)(2,1)}, u32[]{:S(2)}, u32[]{:S(2)}) collective-permute-start(bf16[1,256,256]{2,1,0:T(8,128)(2,1)S(1)} %get-tuple-element.8), channel_id=1, source_target_pairs={{0,2},{2,4},{4,6},{6,8},{8,10},{10,12},{12,14},{1,3},{3,5},{5,7},{... | collective-permute-start | bytes 393224 | tf_op jit(solution)/shard_map/ppermute | solution.py:27
  7.3 7.1 %collective-permute-start.1 = (bf16[1,256,256]{2,1,0:T(8,128)(2,1)}, bf16[1,256,256]{2,1,0:T(8,128)(2,1)S(1)}, u32[]{:S(2)}, u32[]{:S(2)}) collective-permute-start(bf16[1,256,256]{2,1,0:T(8,128)(2,1)} %get-tuple-element.7), channel_id=1, source_target_pairs={{2,0},{4,2},{6,4},{8,6},{10,8},{12,10},{14,12},{3,1},{5,3},{7,5},{... | collective-permute-start | bytes 393224 | tf_op jit(solution)/shard_map/ppermute | solution.py:29
  13.0 4.2 %copy-start.18 = (bf16[256,768]{1,0:T(8,128)(2,1)S(1)}, bf16[256,768]{1,0:T(8,128)(2,1)}, u32[]{:S(2)}) copy-start(bf16[256,768]{1,0:T(8,128)(2,1)} %param.35) | copy-start | bytes 1179652
  13.0 4.2 %copy-start.19 = (bf16[256,768]{1,0:T(8,128)(2,1)S(1)}, bf16[256,768]{1,0:T(8,128)(2,1)}, u32[]{:S(2)}) copy-start(bf16[256,768]{1,0:T(8,128)(2,1)} %param.42) | copy-start | bytes 1179652
  13.1 4.4 %slice-start = ((bf16[256,768]{1,0:T(8,128)(2,1)}), bf16[256,256]{1,0:T(8,128)(2,1)S(1)}, s32[]{:S(2)}) async-start(bf16[256,768]{1,0:T(8,128)(2,1)} %param.35), calls=%async_computation | async-start | bytes 262144 | tf_op jit(solution)/shard_map/slice | solution.py:301
  14.4 3.3 %slice-start.1 = ((bf16[256,768]{1,0:T(8,128)(2,1)}), bf16[256,256]{1,0:T(8,128)(2,1)S(1)}, s32[]{:S(2)}) async-start(bf16[256,768]{1,0:T(8,128)(2,1)} %param.42), calls=%async_computation.1 | async-start | bytes 262144 | tf_op jit(solution)/shard_map/slice | solution.py:301
  14.4 3.8 %collective-permute-start.2 = (bf16[10,1,256]{2,1,0:T(2,128)(2,1)S(1)}, bf16[10,1,256]{2,1,0:T(2,128)(2,1)S(1)}, u32[]{:S(2)}, u32[]{:S(2)}) collective-permute-start(bf16[10,1,256]{2,1,0:T(2,128)(2,1)S(1)} %get-tuple-element.5), channel_id=1, source_target_pairs={{0,1},{2,3},{4,5},{6,7},{8,9},{10,11},{12,13},{14,15},{16,17},{18,... | collective-permute-start | bytes 15368 | tf_op jit(solution)/shard_map/ppermute | solution.py:27
  15.8 3.1 %collective-permute-start.3 = (bf16[10,1,256]{2,1,0:T(2,128)(2,1)S(1)}, bf16[10,1,256]{2,1,0:T(2,128)(2,1)S(1)}, u32[]{:S(2)}, u32[]{:S(2)}) collective-permute-start(bf16[10,1,256]{2,1,0:T(2,128)(2,1)S(1)} %get-tuple-element.6), channel_id=1, source_target_pairs={{1,0},{3,2},{5,4},{7,6},{9,8},{11,10},{13,12},{15,14},{17,16},{19,... | collective-permute-start | bytes 15368 | tf_op jit(solution)/shard_map/ppermute | solution.py:29
  17.2 0.8 copy-start.20
  17.6 2.5 %copy-start.6 = (bf16[256,256]{1,0:T(8,128)(2,1)S(1)}, bf16[256,256]{1,0:T(8,128)(2,1)}, u32[]{:S(2)}) copy-start(bf16[256,256]{1,0:T(8,128)(2,1)} %w_out2.1) | copy-start | bytes 393220
  18.0 2.1 %copy-start.5 = (bf16[256,256]{1,0:T(8,128)(2,1)S(1)}, bf16[256,256]{1,0:T(8,128)(2,1)}, u32[]{:S(2)}) copy-start(bf16[256,256]{1,0:T(8,128)(2,1)} %w_out.1) | copy-start | bytes 393220
  18.0 2.1 %copy-start = (bf16[256,1024]{1,0:T(8,128)(2,1)S(1)}, bf16[256,1024]{1,0:T(8,128)(2,1)}, u32[]{:S(2)}) copy-start(bf16[256,1024]{1,0:T(8,128)(2,1)} %w_expand.1) | copy-start | bytes 1572868
  18.1 2.1 %copy-start.1 = (bf16[1024,256]{1,0:T(8,128)(2,1)S(1)}, bf16[1024,256]{1,0:T(8,128)(2,1)}, u32[]{:S(2)}) copy-start(bf16[1024,256]{1,0:T(8,128)(2,1)} %w_project.1) | copy-start | bytes 1572868
  18.1 2.1 %copy-start.2 = (bf16[256,1024]{1,0:T(8,128)(2,1)S(1)}, bf16[256,1024]{1,0:T(8,128)(2,1)}, u32[]{:S(2)}) copy-start(bf16[256,1024]{1,0:T(8,128)(2,1)} %up.1) | copy-start | bytes 1572868
  18.1 2.1 %copy-start.3 = (bf16[1024,256]{1,0:T(8,128)(2,1)S(1)}, bf16[1024,256]{1,0:T(8,128)(2,1)}, u32[]{:S(2)}) copy-start(bf16[1024,256]{1,0:T(8,128)(2,1)} %down.1) | copy-start | bytes 1572868
  18.1 2.1 %copy-start.4 = (bf16[256,1024]{1,0:T(8,128)(2,1)S(1)}, bf16[256,1024]{1,0:T(8,128)(2,1)}, u32[]{:S(2)}) copy-start(bf16[256,1024]{1,0:T(8,128)(2,1)} %up2.1) | copy-start | bytes 1572868
  18.1 2.1 %copy-start.7 = (f32[1024]{0:T(1024)S(1)}, f32[1024]{0:T(1024)}, u32[]{:S(2)}) copy-start(f32[1024]{0:T(1024)} %param.28) | copy-start | bytes 12292
  18.1 2.1 %copy-start.8 = (f32[1024]{0:T(1024)S(1)}, f32[1024]{0:T(1024)}, u32[]{:S(2)}) copy-start(f32[1024]{0:T(1024)} %param.29) | copy-start | bytes 12292
  18.1 2.1 %copy-start.9 = (f32[1024]{0:T(1024)S(1)}, f32[1024]{0:T(1024)}, u32[]{:S(2)}) copy-start(f32[1024]{0:T(1024)} %param.31) | copy-start | bytes 12292
  18.1 2.1 %copy-start.10 = (f32[1024]{0:T(1024)S(1)}, f32[1024]{0:T(1024)}, u32[]{:S(2)}) copy-start(f32[1024]{0:T(1024)} %param.32) | copy-start | bytes 12292
  18.2 2.1 %copy-start.11 = (f32[256]{0:T(256)S(1)}, f32[256]{0:T(256)}, u32[]{:S(2)}) copy-start(f32[256]{0:T(256)} %param.25) | copy-start | bytes 3076
  18.2 2.1 %copy-start.12 = (f32[256]{0:T(256)S(1)}, f32[256]{0:T(256)}, u32[]{:S(2)}) copy-start(f32[256]{0:T(256)} %param.26) | copy-start | bytes 3076
  18.2 2.1 %copy-start.13 = (f32[256]{0:T(256)S(1)}, f32[256]{0:T(256)}, u32[]{:S(2)}) copy-start(f32[256]{0:T(256)} %param.34) | copy-start | bytes 3076
  18.2 2.1 %copy-start.14 = (f32[256]{0:T(256)S(1)}, f32[256]{0:T(256)}, u32[]{:S(2)}) copy-start(f32[256]{0:T(256)} %param.38) | copy-start | bytes 3076
  18.2 2.0 %copy-start.15 = (f32[256]{0:T(256)S(1)}, f32[256]{0:T(256)}, u32[]{:S(2)}) copy-start(f32[256]{0:T(256)} %param.41) | copy-start | bytes 3076
  18.2 2.0 %copy-start.16 = (f32[256]{0:T(256)S(1)}, f32[256]{0:T(256)}, u32[]{:S(2)}) copy-start(f32[256]{0:T(256)} %param.45) | copy-start | bytes 3076

commit v3 on v2

--- a/solution.py
+++ b/solution.py
@@ -14,23 +14,6 @@
 LOG2E = math.log2(math.e)
 NT = (((1,), (1,)), ((), ()))
 TN = (((0,), (0,)), ((), ()))
-
-
-def extended(cells, sides, width):
-    for axis, dim in sides:
-        count = lax.axis_size(axis)
-        ends = count - 1
-        head = lax.slice_in_dim(cells, 0, width, axis=dim)
-        tail = lax.slice_in_dim(cells, cells.shape[dim] - width, cells.shape[dim], axis=dim)
-        cells = jnp.concatenate(
-            [
-                lax.ppermute(tail, axis, [(i, (i + 1) % count) for i in range(ends)]),
-                cells,
-                lax.ppermute(head, axis, [((i + 1) % count, i) for i in range(ends)]),
-            ],
-            axis=dim,
-        )
-    return cells
 
 
 def biases_keys_first(tables):
@@ -119,14 +102,14 @@
     return total
 
 
-PAD = 8
+PAD = 16
 
 
 def block_kernel(
-    valid, ext, pre_scale, pre_shift, w_expand, ex_scale, ex_shift, taps, dw_scale, dw_shift,
+    weather, pre_scale, pre_shift, w_expand, ex_scale, ex_shift, taps, dw_scale, dw_shift,
     w_project, gain, w_qk, w_vt, w_out, bias, ffgain, up, down, gain2, w_qk2, w_vt2, w_out2,
     bias2, ffgain2, up2, down2, out, grown, depth, one, sent, arrived, returned, back, loose,
-    sent_sem, arrived_sem, returned_sem, back_sem, *, quarter,
+    halo_rows, halo_cols, halo_send, halo_recv, sent_sem, arrived_sem, returned_sem, back_sem, *, quarter,
 ):
     row_at, col_at = lax.axis_index("rows"), lax.axis_index("cols")
     col_count = lax.axis_size("cols")
@@ -149,6 +132,49 @@
         return carry
 
     lax.fori_loop(1, peers, greet, 0)
+    rows, cols, width = out.shape
+    row_count = lax.axis_size("rows")
+
+    def exists(dr, dc):
+        r, c = row_at + dr, col_at + dc
+        return (r >= 0) & (r < row_count) & (c >= 0) & (c < col_count)
+
+    around = [(dr, dc) for dr in (-1, 0, 1) for dc in (-1, 0, 1) if (dr, dc) != (0, 0)]
+
+    def edge_copy(k):
+        dr, dc = around[k]
+        row = {-1: 0, 0: slice(None), 1: rows - 1}[dr]
+        if dc == 0:
+            src, dst = weather.at[row], halo_rows.at[0 if dr > 0 else 1]
+        else:
+            side = 0 if dc > 0 else 1
+            src = weather.at[row, pl.ds(cols - PAD if dc > 0 else 0, PAD)]
+            dst = halo_cols.at[side, {-1: rows + 1, 0: pl.ds(1, rows), 1: 0}[dr]]
+        return pltpu.make_async_remote_copy(
+            src_ref=src, dst_ref=dst, send_sem=halo_send.at[k], recv_sem=halo_recv.at[k],
+            device_id={"rows": row_at + dr, "cols": col_at + dc},
+            device_id_type=pl.DeviceIdType.MESH,
+        )
+
+    greeted = peers - 1
+    for dr, dc in around:
+        if dr != 0 and quarter > 1:
+            greeted = greeted + exists(dr, dc).astype(jnp.int32)
+
+            @pl.when(exists(dr, dc))
+            def _():
+                pl.semaphore_signal(
+                    barrier, 1, device_id={"rows": row_at + dr, "cols": col_at + dc},
+                    device_id_type=pl.DeviceIdType.MESH,
+                )
+
+    pl.semaphore_wait(barrier, greeted)
+    for k, (dr, dc) in enumerate(around):
+
+        @pl.when(exists(dr, dc))
+        def _():
+            edge_copy(k).start()
+
 
     def send(m, src, dst, src_sem, dst_sem):
         def one_peer(k, carry):
@@ -170,48 +196,75 @@
         part = ref.at[m, pl.ds(0, peers - 1)]
         pltpu.make_async_copy(part, part, sem.at[m]).wait()
 
-    rows, cols, width = out.shape
     wide = w_expand.shape[1]
-    span = ext.shape[1]
-    column = lax.broadcasted_iota(jnp.int32, (span, 1), 0)
-    edge = jnp.where(column == PAD - 1, valid[2], jnp.where(column == PAD + cols, valid[3], 1.0))
-
-    def expand(r, carry):
-        keep = jnp.where(r == 0, valid[0], jnp.where(r == rows + 1, valid[1], 1.0))
-        x = (ext[r].astype(F32) * pre_scale[...] + pre_shift[...]).astype(BF)
+
+    def grow(x, store):
+        x = (x.astype(F32) * pre_scale[...] + pre_shift[...]).astype(BF)
         for at in range(0, wide, 256):
             s = slice(at, at + 256)
-            y = gelu(dot(x, w_expand[:, s]) * ex_scale[:, s] + ex_shift[:, s])
-            grown[r, :, s] = (y * (edge * keep)).astype(BF)
-        return carry
-
-    lax.fori_loop(0, rows + 2, expand, 0)
-
-    def row(r, carry):
-        for lane in range(0, wide, 128):
-            ls = slice(lane, lane + 128)
-            for c in range(0, cols, 64):
+            store(s, gelu(dot(x, w_expand[:, s]) * ex_scale[:, s] + ex_shift[:, s]))
+
+    def expand(r, carry):
+        def store(s, y):
+            grown[r + 1, PAD : PAD + cols, s] = y.astype(BF)
+
+        grow(weather[r], store)
+        return carry
+
+    lax.fori_loop(0, rows, expand, 0)
+    for k, (dr, dc) in enumerate(around):
+
+        @pl.when(exists(-dr, -dc))
+        def _():
+            edge_copy(k).wait_recv()
+
+    def expand_row(d, carry):
+        keep = jnp.where(d == 0, row_at, row_count - 1 - row_at) > 0
+
+        def store(s, y):
+            grown[d * (rows + 1), PAD : PAD + cols, s] = jnp.where(keep, y, 0.0).astype(BF)
+
+        grow(halo_rows[d], store)
+        return carry
+
+    lax.fori_loop(0, 2, expand_row, 0)
+    line = lax.broadcasted_iota(jnp.int32, ((rows + 2) * PAD, 256), 0) // PAD
+    inside = ((line > 0) | (row_at > 0)) & ((line < rows + 1) | (row_at < row_count - 1))
+    for side in range(2):
+        keep = inside & ((col_at > 0) if side == 0 else (col_at < col_count - 1))
+
+        def store(s, y):
+            y = jnp.where(keep, y, 0.0).astype(BF).reshape(rows + 2, PAD, 256)
+            grown[:, (PAD + cols) * side : (PAD + cols) * side + PAD, s] = y
+
+        grow(halo_cols[side].reshape((rows + 2) * PAD, width), store)
+
+    strip = cols // 8
+
+    def row(step, carry):
+        part, r = step // rows, lax.rem(step, rows)
+        for g in range(4):
+            c = pl.multiple_of(g * 2 * strip + part * strip, 16)
+            for lane in range(0, wide, 128):
+                ls = slice(lane, lane + 128)
                 sums = [None] * 3
                 for a in range(3):
-                    e = grown[r + a, c : c + 64 + 2 * PAD, ls].astype(F32)
+                    e = grown[r + a, pl.ds(c, strip + 2 * PAD), ls].astype(F32)
+                    e = e[PAD - 8 : PAD + strip + 8]
                     for b in range(3):
                         term = e * taps[3 * a + b : 3 * a + b + 1, ls]
                         sums[b] = term if a == 0 else sums[b] + term
-                total = (
-                    sums[0][PAD - 1 : PAD + 63]
-                    + sums[1][PAD : PAD + 64]
-                    + sums[2][PAD + 1 : PAD + 65]
-                )
-                depth[c : c + 64, ls] = gelu(
+                total = sums[0][7 : 7 + strip] + sums[1][8 : 8 + strip] + sums[2][9 : 9 + strip]
+                depth[strip * g : strip * (g + 1), ls] = gelu(
                     total * dw_scale[:, ls] + dw_shift[:, ls]
                 ).astype(BF)
-        y = ext[r + 1, PAD : PAD + cols, :].astype(F32) + dot(depth[...], w_project[...])
-        one[r] = y.astype(BF).astype(F32)
-        return carry
-
-    lax.fori_loop(0, rows, row, 0)
-
-    pl.semaphore_wait(barrier, peers - 1)
+        y = dot(depth[...], w_project[...])
+        for g in range(4):
+            c = pl.multiple_of(g * 2 * strip + part * strip, 16)
+            z = weather[r, pl.ds(c, strip), :].astype(F32) + y[strip * g : strip * (g + 1)]
+            one[r, pl.ds(c, strip), :] = z.astype(BF).astype(F32)
+        return carry
+
     first_half = lax.rem(lax.broadcasted_iota(jnp.int32, (WIN * WIN, width), 0), WIN) < WIN // 2
     half = WIN // 2
     chunks = cols // 32
@@ -240,7 +293,12 @@
         send(m, sent, arrived, sent_sem, arrived_sem)
         return carry
 
-    lax.fori_loop(0, chunks, window, 0)
+    def part(p, carry):
+        lax.fori_loop(p * rows, (p + 1) * rows, row, 0)
+        lax.fori_loop(p * (chunks // 2), (p + 1) * (chunks // 2), window, 0)
+        return carry
+
+    lax.fori_loop(0, 2, part, 0)
 
     def group(m, carry):
         wait_all(m, arrived, arrived_sem)
@@ -291,6 +349,11 @@
         return carry
 
     lax.fori_loop(0, chunks, drain, 0)
+    for k, (dr, dc) in enumerate(around):
+
+        @pl.when(exists(dr, dc))
+        def _():
+            edge_copy(k).wait_send()
 
 
 def attention_operands(gain, w_qkv, w_out, bias):
@@ -314,10 +377,6 @@
     side = WIN
     rows_count = lax.axis_size("rows")
     cols_count = lax.axis_size("cols")
-    ext = extended(weather, (("rows", 0), ("cols", 1)), 1)
-    ext = jnp.pad(ext, ((0, 0), (PAD - 1, PAD - 1), (0, 0)))
-    ri, ci = lax.axis_index("rows"), lax.axis_index("cols")
-    valid = jnp.stack([ri > 0, ri < rows_count - 1, ci > 0, ci < cols_count - 1]).astype(F32)
     vmem = pl.BlockSpec(memory_space=pltpu.VMEM)
     biases = biases_keys_first(jnp.stack([win_table, grid_table]))
     chunks = tile_cols // 32
@@ -325,17 +384,21 @@
     return pl.pallas_call(
         functools.partial(block_kernel, quarter=rows_count // side),
         out_shape=jax.ShapeDtypeStruct((tile_rows, tile_cols, width), BF),
-        in_specs=[pl.BlockSpec(memory_space=pltpu.SMEM)] + [vmem] * 26,
+        in_specs=[vmem] * 26,
         out_specs=vmem,
         scratch_shapes=[
             pltpu.VMEM((tile_rows + 2, tile_cols + 2 * PAD, wide), BF),
-            pltpu.VMEM((tile_cols, wide), BF),
+            pltpu.VMEM((tile_cols // 2, wide), BF),
             pltpu.VMEM((tile_rows, tile_cols, width), F32),
             slots,
             slots,
             slots,
             slots,
             pltpu.VMEM((width // 128, 256, 128), F32),
+            pltpu.VMEM((2, tile_cols, width), BF),
+            pltpu.VMEM((2, tile_rows + 2, PAD, width), BF),
+            pltpu.SemaphoreType.DMA((8,)),
+            pltpu.SemaphoreType.DMA((8,)),
         ]
         + [pltpu.SemaphoreType.DMA((chunks,))] * 4,
         compiler_params=pltpu.CompilerParams(
@@ -343,7 +406,7 @@
         ),
         name="maxvit",
     )(
-        valid, ext, pre_scale[None], pre_shift[None], w_expand, ex_scale[None], ex_shift[None],
+        weather, pre_scale[None], pre_shift[None], w_expand, ex_scale[None], ex_shift[None],
         dw_kernel.reshape(9, wide), dw_scale[None], dw_shift[None], w_project,
         *attention_operands(win_gain, win_qkv, win_out, biases[0]),
         winff_gain[None], winff_up, winff_down,

time: 98.8 us -> 92.6 us (0.937)
  starting transfers between devices: 9.64 us -> 0 us
  Pallas kernels: 75.8 us -> 80.8 us
  local copies, waits for them, and re-layouts: 5.84 us -> 8.43 us
  waiting for transfers between devices: 1.89 us -> 0 us
  other arithmetic: 1.4 us -> 0.09 us
    ppermute x4 -> x0, starting transfers between devices: 9.64 us -> none  [the longest x2 7.07 us: extended(): lax.ppermute(tail, axis, [(i, (i + 1) % count) for i in range(ends)])]
    pallas_call x1, Pallas kernels: 75.8 us -> 80.8 us  [local(): pl.pallas_call(functools.partial(block_kernel, quarter=rows_count // side...]
    ppermute x4 -> x0, waiting for transfers between devices: 1.89 us -> none  [the longest x2 1.88 us: extended(): lax.ppermute(head, axis, [((i + 1) % count, i) for i in range(ends)])]
    slice x2 -> x0, local copies, waits for them, and re-layouts: 1.66 us -> none  [the longest x1 1.64 us: extended(): head = lax.slice_in_dim(cells, 0, width, axis=dim)]
    concatenate x1 -> x0, other arithmetic: 1.22 us -> none  [extended(): jnp.concatenate([lax.ppermute(tail, axis, [(i, (i + 1) % count) for i in...]
    unnamed x47 -> x45, local copies, waits for them, and re-layouts: 3.83 us -> 3.62 us
  transfers between devices with their start and end apart: 4 -> 0, of which waited for: 2 -> 0; matrix products, arithmetic and copies ran while one was open for 5% -> 0% of each run, Pallas kernels for 0% -> 0%
where the time goes in v3:
time: 92.6 us; the launch traced here: 92.3 us
  Pallas kernels  80.8 us (87%)
  local copies, waits for them, and re-layouts  8.43 us (9%)
  matrix products  2.62 us (3%)
    pallas_call x1, Pallas kernels, local(): pl.pallas_call(functools.partial(block_kernel, quarter=rows_count // side...  80.8 us
    unnamed x45, local copies, waits for them, and re-layouts  3.62 us
    dot_general x1, matrix products, biases_keys_first(): jnp.dot(tables.reshape(count * heads, offsets) * LOG2E, onehot, precision...  2.62 us

profile of v3, /device:TPU:0, one launch (start us, length us, event | category | flops | bytes accessed | tf_op | source)
XLA Modules:
  0.0 92.3 jit_solution(12862702685031828263)
XLA Ops:
  0.0 0.1 fusion.10
  0.1 0.9 reshape.98.taps
  1.0 0.0 copy-start.19
  1.0 0.0 copy-start.20
  1.0 0.9 %slice.21 = bf16[256,256]{1,0:T(8,128)(2,1)S(1)} slice(bf16[256,768]{1,0:T(8,128)(2,1)} %param.35), slice={[0:256], [512:768]} | slice | bytes 262144 | tf_op jit(solution)/shard_map/slice | solution.py:364
  2.0 0.1 copy.28
  2.1 0.0 slice-done
  2.1 0.1 copy.29
  2.2 0.0 copy-done.18
  2.3 0.0 copy-start.3
  2.3 0.0 copy-start.7
  2.3 0.0 copy-start.8
  2.3 0.0 copy-start.9
  2.3 0.0 copy-start.10
  2.3 0.0 copy-start.14
  2.3 0.0 copy-start.15
  2.4 0.0 copy-start.16
  2.4 2.6 %fusion.4 = f32[2,64,8,64]{3,2,1,0:T(8,128)S(1)} fusion(s32[64,64]{1,0:T(8,128)S(1)} %fusion.10, f32[1,8,225]{2,1,0:T(8,128)S(1)} %bitcast.42, f32[1,8,225]{2,1,0:T(8,128)S(1)} %bitcast.43), kind=kOutput, calls=%fused_computation.4 | convolution fusion | flops 177876000 | bytes 292928 | tf_op jit(solution)/shard_map/dot_general | solution.py:26
  5.0 0.0 copy-start.1
  5.0 0.0 copy-start.2
  5.0 0.0 copy-start.5
  5.0 0.0 copy-start.6
  5.0 0.0 copy-start.11
  5.0 0.0 copy-start.12
  5.1 0.0 copy-start.13
  5.1 0.8 fusion.35
  5.9 1.1 %squeeze.7.bias2 = f32[64,512]{1,0:T(8,128)S(1)} reshape(f32[1,64,8,64]{3,2,1,0:T(8,128)} %get-tuple-element.5) | data formatting | bytes 262144 | tf_op jit(solution)/shard_map/squeeze | solution.py:413
  7.0 1.1 %squeeze.6.bias = f32[64,512]{1,0:T(8,128)S(1)} reshape(f32[1,64,8,64]{3,2,1,0:T(8,128)} %get-tuple-element.6) | data formatting | bytes 262144 | tf_op jit(solution)/shard_map/squeeze | solution.py:411
  8.2 0.0 copy-start.4
  8.2 1.0 %copy-done.4 = bf16[256,1024]{1,0:T(8,128)(2,1)S(1)} copy-done((bf16[256,1024]{1,0:T(8,128)(2,1)S(1)}, bf16[256,1024]{1,0:T(8,128)(2,1)}, u32[]{:S(2)}) %copy-start.4) | copy-done | bytes 524312
  9.2 80.8 %maxvit.1 = bf16[8,256,256]{2,1,0:T(8,128)(2,1)} custom-call(bf16[8,256,256]{2,1,0:T(8,128)(2,1)} %weather.1, f32[1,256]{1,0:T(1,128)S(1)} %bitcast.36, f32[1,256]{1,0:T(1,128)S(1)} %bitcast.37, bf16[256,1024]{1,0:T(8,128)(2,1)S(1)} %copy-done, f32[1,1024]{1,0:T(1,128)S(1)} %bitcast.32, f32[1,1024]{1,0:T(1,128)S(1)} %bitcast.33, ...), custom_call_target="tpu_custom_call" | custom-call | tf_op jit(solution)/shard_map/maxvit/pallas_call | solution.py:384
  90.0 2.3 %copy.31 = bf16[8,256,256]{2,1,0:T(8,128)(2,1)} copy(bf16[8,256,256]{2,1,0:T(8,128)(2,1)} %maxvit.1) | data formatting | bytes 2097152
  (25 shorter events, 0.1 us)
Async XLA Ops:
  0.0 2.1 %slice-start = ((bf16[256,768]{1,0:T(8,128)(2,1)}), bf16[256,256]{1,0:T(8,128)(2,1)S(1)}, s32[]{:S(2)}) async-start(bf16[256,768]{1,0:T(8,128)(2,1)} %param.42), calls=%async_computation | async-start | bytes 262144 | tf_op jit(solution)/shard_map/slice | solution.py:364
  0.0 2.2 %copy-start.17 = (bf16[256,768]{1,0:T(8,128)(2,1)S(1)}, bf16[256,768]{1,0:T(8,128)(2,1)}, u32[]{:S(2)}) copy-start(bf16[256,768]{1,0:T(8,128)(2,1)} %param.42) | copy-start | bytes 1179652
  0.0 2.2 %copy-start.18 = (bf16[256,768]{1,0:T(8,128)(2,1)S(1)}, bf16[256,768]{1,0:T(8,128)(2,1)}, u32[]{:S(2)}) copy-start(bf16[256,768]{1,0:T(8,128)(2,1)} %param.35) | copy-start | bytes 1179652
  1.0 1.2 %copy-start.19 = (f32[8,225]{1,0:T(8,128)S(1)}, f32[8,225]{1,0:T(8,128)}, u32[]{:S(2)}) copy-start(f32[8,225]{1,0:T(8,128)} %param.44) | copy-start | bytes 21604
  1.0 1.2 %copy-start.20 = (f32[8,225]{1,0:T(8,128)S(1)}, f32[8,225]{1,0:T(8,128)}, u32[]{:S(2)}) copy-start(f32[8,225]{1,0:T(8,128)} %param.37) | copy-start | bytes 21604
  2.3 5.8 %copy-start.3 = (bf16[1024,256]{1,0:T(8,128)(2,1)S(1)}, bf16[1024,256]{1,0:T(8,128)(2,1)}, u32[]{:S(2)}) copy-start(bf16[1024,256]{1,0:T(8,128)(2,1)} %down.1) | copy-start | bytes 1572868
  2.3 5.8 %copy-start.7 = (f32[1024]{0:T(1024)S(1)}, f32[1024]{0:T(1024)}, u32[]{:S(2)}) copy-start(f32[1024]{0:T(1024)} %param.28) | copy-start | bytes 12292
  2.3 5.7 %copy-start.8 = (f32[1024]{0:T(1024)S(1)}, f32[1024]{0:T(1024)}, u32[]{:S(2)}) copy-start(f32[1024]{0:T(1024)} %param.29) | copy-start | bytes 12292
  2.3 5.7 %copy-start.9 = (f32[1024]{0:T(1024)S(1)}, f32[1024]{0:T(1024)}, u32[]{:S(2)}) copy-start(f32[1024]{0:T(1024)} %param.31) | copy-start | bytes 12292
  2.3 5.7 %copy-start.10 = (f32[1024]{0:T(1024)S(1)}, f32[1024]{0:T(1024)}, u32[]{:S(2)}) copy-start(f32[1024]{0:T(1024)} %param.32) | copy-start | bytes 12292
  2.3 5.7 %copy-start.14 = (f32[256]{0:T(256)S(1)}, f32[256]{0:T(256)}, u32[]{:S(2)}) copy-start(f32[256]{0:T(256)} %param.38) | copy-start | bytes 3076
  2.3 5.7 %copy-start.15 = (f32[256]{0:T(256)S(1)}, f32[256]{0:T(256)}, u32[]{:S(2)}) copy-start(f32[256]{0:T(256)} %param.41) | copy-start | bytes 3076
  2.4 5.7 %copy-start.16 = (f32[256]{0:T(256)S(1)}, f32[256]{0:T(256)}, u32[]{:S(2)}) copy-start(f32[256]{0:T(256)} %param.45) | copy-start | bytes 3076
  5.0 3.1 %copy-start = (bf16[256,1024]{1,0:T(8,128)(2,1)S(1)}, bf16[256,1024]{1,0:T(8,128)(2,1)}, u32[]{:S(2)}) copy-start(bf16[256,1024]{1,0:T(8,128)(2,1)} %w_expand.1) | copy-start | bytes 1572868
  5.0 3.1 %copy-start.1 = (bf16[1024,256]{1,0:T(8,128)(2,1)S(1)}, bf16[1024,256]{1,0:T(8,128)(2,1)}, u32[]{:S(2)}) copy-start(bf16[1024,256]{1,0:T(8,128)(2,1)} %w_project.1) | copy-start | bytes 1572868
  5.0 3.1 %copy-start.2 = (bf16[256,1024]{1,0:T(8,128)(2,1)S(1)}, bf16[256,1024]{1,0:T(8,128)(2,1)}, u32[]{:S(2)}) copy-start(bf16[256,1024]{1,0:T(8,128)(2,1)} %up.1) | copy-start | bytes 1572868
  5.0 3.1 %copy-start.5 = (bf16[256,256]{1,0:T(8,128)(2,1)S(1)}, bf16[256,256]{1,0:T(8,128)(2,1)}, u32[]{:S(2)}) copy-start(bf16[256,256]{1,0:T(8,128)(2,1)} %w_out.1) | copy-start | bytes 393220
  5.0 3.1 %copy-start.6 = (bf16[256,256]{1,0:T(8,128)(2,1)S(1)}, bf16[256,256]{1,0:T(8,128)(2,1)}, u32[]{:S(2)}) copy-start(bf16[256,256]{1,0:T(8,128)(2,1)} %w_out2.1) | copy-start | bytes 393220
  5.0 3.1 %copy-start.11 = (f32[256]{0:T(256)S(1)}, f32[256]{0:T(256)}, u32[]{:S(2)}) copy-start(f32[256]{0:T(256)} %param.25) | copy-start | bytes 3076
  5.0 3.1 %copy-start.12 = (f32[256]{0:T(256)S(1)}, f32[256]{0:T(256)}, u32[]{:S(2)}) copy-start(f32[256]{0:T(256)} %param.26) | copy-start | bytes 3076
  5.1 3.1 %copy-start.13 = (f32[256]{0:T(256)S(1)}, f32[256]{0:T(256)}, u32[]{:S(2)}) copy-start(f32[256]{0:T(256)} %param.34) | copy-start | bytes 3076
  8.2 1.0 %copy-start.4 = (bf16[256,1024]{1,0:T(8,128)(2,1)S(1)}, bf16[256,1024]{1,0:T(8,128)(2,1)}, u32[]{:S(2)}) copy-start(bf16[256,1024]{1,0:T(8,128)(2,1)} %up2.1) | copy-start | bytes 1572868

commit v4 on v3

--- a/solution.py
+++ b/solution.py
@@ -252,7 +252,7 @@
                     e = grown[r + a, pl.ds(c, strip + 2 * PAD), ls].astype(F32)
                     e = e[PAD - 8 : PAD + strip + 8]
                     for b in range(3):
-                        term = e * taps[3 * a + b : 3 * a + b + 1, ls]
+                        term = e * taps[a, b : b + 1, ls]
                         sums[b] = term if a == 0 else sums[b] + term
                 total = sums[0][7 : 7 + strip] + sums[1][8 : 8 + strip] + sums[2][9 : 9 + strip]
                 depth[strip * g : strip * (g + 1), ls] = gelu(
@@ -280,7 +280,7 @@
             at = pl.multiple_of(g * (cols // 4) + m * WIN, WIN)
             pieces.append(one[:, pl.ds(at, WIN), :].reshape(WIN * WIN, width))
         x = jnp.concatenate(pieces, axis=0)
-        x = attend(x, gain[...], w_qk[...], w_vt[...], w_out[...], bias[...])
+        x = attend(x, gain[...], w_qk[:, : 2 * width], w_vt[...], w_out[...], bias[0])
         x = feed(x, ffgain[...], up, down)
         x = [x[WIN * WIN * g : WIN * WIN * (g + 1)] for g in range(4)]
         low, high = exchange(x[0], x[1]), exchange(x[2], x[3])
@@ -312,7 +312,7 @@
             ],
             axis=0,
         )
-        x = attend(x, gain2[...], w_qk2[...], w_vt2[...], w_out2[...], bias2[...])
+        x = attend(x, gain2[...], w_qk2[:, : 2 * width], w_vt2[...], w_out2[...], bias2[1])
         x = feed(x, ffgain2[...], up2, down2)
         for g in range(4):
             for h in range(width // 128):
@@ -360,7 +360,7 @@
     width = w_qkv.shape[0]
     return (
         gain[None],
-        w_qkv[:, : 2 * width],
+        w_qkv,
         w_qkv[:, 2 * width :].T,
         w_out,
         bias,
@@ -407,10 +407,10 @@
         name="maxvit",
     )(
         weather, pre_scale[None], pre_shift[None], w_expand, ex_scale[None], ex_shift[None],
-        dw_kernel.reshape(9, wide), dw_scale[None], dw_shift[None], w_project,
-        *attention_operands(win_gain, win_qkv, win_out, biases[0]),
+        dw_kernel, dw_scale[None], dw_shift[None], w_project,
+        *attention_operands(win_gain, win_qkv, win_out, biases),
         winff_gain[None], winff_up, winff_down,
-        *attention_operands(grid_gain, grid_qkv, grid_out, biases[1]),
+        *attention_operands(grid_gain, grid_qkv, grid_out, biases),
         gridff_gain[None], gridff_up, gridff_down,
     )
 

time: 92.6 us -> 96.7 us (1.044)
  local copies, waits for them, and re-layouts: 8.43 us -> 11.5 us
    unnamed x45, local copies, waits for them, and re-layouts: 3.62 us -> 8.31 us
    squeeze x2 -> x0, local copies, waits for them, and re-layouts: 2.13 us -> none  [the longest x1 1.06 us: local(): biases[1]]
    slice x6 -> x2, local copies, waits for them, and re-layouts: 1.78 us -> 1.95 us  [attention_operands(): return (gain[None], w_qkv, w_qkv[:, 2 * width:].T, w_out, bias)]
where the time goes in v4:
time: 96.7 us; the launch traced here: 96.3 us
  Pallas kernels  81 us (84%)
  local copies, waits for them, and re-layouts  11.5 us (12%)
  matrix products  3.55 us (4%)
    pallas_call x1, Pallas kernels, local(): pl.pallas_call(functools.partial(block_kernel, quarter=rows_count // side...  81 us
    unnamed x45, local copies, waits for them, and re-layouts  8.31 us
    dot_general x1, matrix products, biases_keys_first(): jnp.dot(tables.reshape(count * heads, offsets) * LOG2E, onehot, precision...  3.55 us
    slice x2, local copies, waits for them, and re-layouts, attention_operands(): return (gain[None], w_qkv, w_qkv[:, 2 * width:].T, w_out, bias)  1.95 us

profile of v4, /device:TPU:0, one launch (start us, length us, event | category | flops | bytes accessed | tf_op | source)
XLA Modules:
  0.0 96.3 jit_solution(2477012448663165547)
XLA Ops:
  0.0 0.1 fusion.10
  0.1 0.0 copy-start.5
  0.1 1.0 %slice.6 = bf16[256,256]{1,0:T(8,128)(2,1)S(1)} slice(bf16[256,768]{1,0:T(8,128)(2,1)} %w_qk.1), slice={[0:256], [512:768]} | slice | bytes 262144 | tf_op jit(solution)/shard_map/slice | solution.py:364
  1.1 0.1 copy.28
  1.2 0.0 copy-start.4
  1.2 1.0 %slice.7 = bf16[256,256]{1,0:T(8,128)(2,1)S(1)} slice(bf16[256,768]{1,0:T(8,128)(2,1)} %w_qk2.1), slice={[0:256], [512:768]} | slice | bytes 262144 | tf_op jit(solution)/shard_map/slice | solution.py:364
  2.2 0.1 copy.29
  2.3 0.0 copy-start
  2.3 0.0 copy-start.1
  2.3 0.0 copy-start.2
  2.3 0.0 copy-start.3
  2.3 0.0 copy-start.6
  2.4 0.0 copy-start.9
  2.4 0.0 copy-start.10
  2.4 0.0 copy-start.11
  2.4 0.0 copy-start.12
  2.4 0.0 copy-done.19
  2.4 0.0 copy-done.20
  2.4 3.5 %fusion.4 = f32[2,64,8,64]{3,2,1,0:T(8,128)} fusion(s32[64,64]{1,0:T(8,128)S(1)} %fusion.10, f32[1,8,225]{2,1,0:T(8,128)S(1)} %bitcast.40, f32[1,8,225]{2,1,0:T(8,128)S(1)} %bitcast.41), kind=kOutput, calls=%fused_computation.4 | convolution fusion | flops 177876000 | bytes 292928 | tf_op jit(solution)/shard_map/dot_general | solution.py:26
  6.0 1.2 %reshape.93.bias.bias2 = f32[2,64,512]{2,1,0:T(8,128)S(1)} reshape(f32[2,64,8,64]{3,2,1,0:T(8,128)} %fusion.4) | data formatting | bytes 524288 | tf_op jit(solution)/shard_map/reshape | solution.py:30
  7.2 0.0 copy-done.5
  7.3 0.0 copy-start.7
  7.3 0.9 copy-done.7
  8.2 0.8 copy-done.8
  9.0 0.7 copy-done.13
  9.7 0.7 copy-done.14
  10.4 0.7 copy-done.15
  11.0 0.7 copy-done.16
  11.7 0.7 copy-done.17
  12.4 0.7 copy-done.18
  13.1 81.0 %maxvit.1 = bf16[8,256,256]{2,1,0:T(8,128)(2,1)} custom-call(bf16[8,256,256]{2,1,0:T(8,128)(2,1)} %weather.1, f32[1,256]{1,0:T(1,128)S(1)} %bitcast.34, f32[1,256]{1,0:T(1,128)S(1)} %bitcast.35, bf16[256,1024]{1,0:T(8,128)(2,1)S(1)} %copy-done.2, f32[1,1024]{1,0:T(1,128)S(1)} %bitcast.30, f32[1,1024]{1,0:T(1,128)S(1)} %bitcast.31, ...), custom_call_target="tpu_custom_call" | custom-call | tf_op jit(solution)/shard_map/maxvit/pallas_call | solution.py:384
  94.0 2.3 %copy.31 = bf16[8,256,256]{2,1,0:T(8,128)(2,1)} copy(bf16[8,256,256]{2,1,0:T(8,128)(2,1)} %maxvit.1) | data formatting | bytes 2097152
  (19 shorter events, 0.0 us)
Async XLA Ops:
  0.0 2.4 %copy-start.19 = (f32[8,225]{1,0:T(8,128)S(1)}, f32[8,225]{1,0:T(8,128)}, u32[]{:S(2)}) copy-start(f32[8,225]{1,0:T(8,128)} %param.44) | copy-start | bytes 21604
  0.0 2.4 %copy-start.20 = (f32[8,225]{1,0:T(8,128)S(1)}, f32[8,225]{1,0:T(8,128)}, u32[]{:S(2)}) copy-start(f32[8,225]{1,0:T(8,128)} %param.37) | copy-start | bytes 21604
  0.1 7.1 %copy-start.5 = (bf16[1024,256]{1,0:T(8,128)(2,1)S(1)}, bf16[1024,256]{1,0:T(8,128)(2,1)}, u32[]{:S(2)}) copy-start(bf16[1024,256]{1,0:T(8,128)(2,1)} %down.1) | copy-start | bytes 1572868
  1.2 6.0 %copy-start.4 = (bf16[256,1024]{1,0:T(8,128)(2,1)S(1)}, bf16[256,1024]{1,0:T(8,128)(2,1)}, u32[]{:S(2)}) copy-start(bf16[256,1024]{1,0:T(8,128)(2,1)} %up.1) | copy-start | bytes 1572868
  2.3 4.9 %copy-start = (bf16[256,768]{1,0:T(8,128)(2,1)S(1)}, bf16[256,768]{1,0:T(8,128)(2,1)}, u32[]{:S(2)}) copy-start(bf16[256,768]{1,0:T(8,128)(2,1)} %w_qk.1) | copy-start | bytes 1179652
  2.3 4.9 %copy-start.1 = (bf16[256,768]{1,0:T(8,128)(2,1)S(1)}, bf16[256,768]{1,0:T(8,128)(2,1)}, u32[]{:S(2)}) copy-start(bf16[256,768]{1,0:T(8,128)(2,1)} %w_qk2.1) | copy-start | bytes 1179652
  2.3 4.9 %copy-start.2 = (bf16[256,1024]{1,0:T(8,128)(2,1)S(1)}, bf16[256,1024]{1,0:T(8,128)(2,1)}, u32[]{:S(2)}) copy-start(bf16[256,1024]{1,0:T(8,128)(2,1)} %w_expand.1) | copy-start | bytes 1572868
  2.3 4.9 %copy-start.3 = (bf16[1024,256]{1,0:T(8,128)(2,1)S(1)}, bf16[1024,256]{1,0:T(8,128)(2,1)}, u32[]{:S(2)}) copy-start(bf16[1024,256]{1,0:T(8,128)(2,1)} %w_project.1) | copy-start | bytes 1572868
  2.3 4.9 %copy-start.6 = (bf16[256,256]{1,0:T(8,128)(2,1)S(1)}, bf16[256,256]{1,0:T(8,128)(2,1)}, u32[]{:S(2)}) copy-start(bf16[256,256]{1,0:T(8,128)(2,1)} %w_out.1) | copy-start | bytes 393220
  2.4 4.9 %copy-start.9 = (f32[1024]{0:T(1024)S(1)}, f32[1024]{0:T(1024)}, u32[]{:S(2)}) copy-start(f32[1024]{0:T(1024)} %param.28) | copy-start | bytes 12292
  2.4 4.9 %copy-start.10 = (f32[1024]{0:T(1024)S(1)}, f32[1024]{0:T(1024)}, u32[]{:S(2)}) copy-start(f32[1024]{0:T(1024)} %param.29) | copy-start | bytes 12292
  2.4 4.9 %copy-start.11 = (f32[1024]{0:T(1024)S(1)}, f32[1024]{0:T(1024)}, u32[]{:S(2)}) copy-start(f32[1024]{0:T(1024)} %param.31) | copy-start | bytes 12292
  2.4 4.9 %copy-start.12 = (f32[1024]{0:T(1024)S(1)}, f32[1024]{0:T(1024)}, u32[]{:S(2)}) copy-start(f32[1024]{0:T(1024)} %param.32) | copy-start | bytes 12292
  7.3 0.9 copy-start.7
  8.2 0.8 copy-start.8
  9.0 0.7 copy-start.13
  9.7 0.7 copy-start.14
  10.3 0.7 copy-start.15
  11.0 0.7 copy-start.16
  11.7 0.7 copy-start.17
  12.4 0.7 copy-start.18
